TPU v7x, 32 devices: a whole 2x2x4 slice. The times are simulated.
32 devices in a mesh: groups: 2 (over x), tile: 16 (over z, y, core).
Axes of the slice: x: 2, y: 2, z: 4, core: 2. Of those that a mesh axis runs over, the one named last changes fastest.
Arguments:
- grid_latent: bfloat16 [32768, 512], P(('groups', 'tile')), parts along dimension 0, may hold values from -6 to 6
- mesh_latent: bfloat16 [8192, 512], P(('groups', 'tile')), parts along dimension 0, may hold values from -6 to 6
- enc_feats: float32 [4, 65536], P(None, ('groups', 'tile')), parts along dimension 1, may hold values from -6 to 6
- enc_sender: int32 [65536], P(('groups', 'tile')), parts along dimension 0, may hold values from 0 to 1535, as said below
- enc_receiver: int32 [65536], P(('groups', 'tile')), parts along dimension 0, may hold values from 0 to 255
- enc_count: int32 [32], P(('groups', 'tile')), parts along dimension 0, may hold values from 1024 to 2048
- mesh_feats: float32 [4, 65536], P(None, ('groups', 'tile')), parts along dimension 1, may hold values from -6 to 6
- mesh_sender: int32 [65536], P(('groups', 'tile')), parts along dimension 0, may hold values from 0 to 255, as said below
- mesh_receiver: int32 [65536], P(('groups', 'tile')), parts along dimension 0, may hold values from 0 to 255
- mesh_count: int32 [32], P(('groups', 'tile')), parts along dimension 0, may hold values from 1024 to 2048
- need_rows: int32 [32, 16, 16], P(('groups', 'tile')), parts along dimension 0, may hold values from 0 to 255, as said below
- w_enc_feat: float32 [4, 512], replicated, may hold values from -3 to 3
- w_enc_send: bfloat16 [512, 512], replicated, may hold values from -0.25 to 0.25
- w_enc_recv: bfloat16 [512, 512], replicated, may hold values from -0.25 to 0.25
- w_enc_out: bfloat16 [512, 512], replicated, may hold values from -0.25 to 0.25
- w_enc_node_in: bfloat16 [1024, 512], replicated, may hold values from -0.1875 to 0.1875
- w_enc_node_out: bfloat16 [512, 512], replicated, may hold values from -0.25 to 0.25
- w_proc_feat: float32 [4, 512], replicated, may hold values from -3 to 3
- w_proc_send: bfloat16 [512, 512], replicated, may hold values from -0.25 to 0.25
- w_proc_recv: bfloat16 [512, 512], replicated, may hold values from -0.25 to 0.25
- w_proc_out: bfloat16 [512, 512], replicated, may hold values from -0.25 to 0.25
- w_proc_node_in: bfloat16 [1024, 512], replicated, may hold values from -0.1875 to 0.1875
- w_proc_node_out: bfloat16 [512, 512], replicated, may hold values from -0.25 to 0.25
Outputs:
- mesh_out: bfloat16 [8192, 512], P(('groups', 'tile')), parts along dimension 0
There are 2 independent parts, one for each index of `groups`. A program takes and returns all parts, laid end to end along the dimension named above; an argument that names none is the same for every part. Nothing has to cross between parts.
Inputs may be any that keep to these rules, and one draw needn't show every extreme that they name: `enc_sender`: in block 0 every entry is 256 or more, in the last block every entry is under 1024 + 256; so no edge starts outside the grid. `mesh_sender`: entry p * 16 + s names need_rows[b, p, s] of the slot's own block b. `need_rows`: the 16 entries of each list are distinct.
All inputs are finite; a program needn't handle non-finite values.
Results may differ from a plain program's by a relative error of at most 0.009.
Values may be sent and summed in bfloat16 or wider, within the bound.
No kernel may reach another device: no remote copies, remote signals or barrier semaphores. Data moves between devices by JAX's collectives and lax.ppermute only.
A program may use at most 64 MiB of HBM per device.

v0:
```python
import jax
import jax.numpy as jnp
from jax import lax
from jax.sharding import PartitionSpec as P

HALO = 256


def padded(cells, sides, width):
    for axis, dim in sides:
        count = lax.axis_size(axis)
        ends = count - 1
        head = lax.slice_in_dim(cells, 0, width, axis=dim)
        tail = lax.slice_in_dim(cells, cells.shape[dim] - width, cells.shape[dim], axis=dim)
        cells = jnp.concatenate(
            [
                lax.ppermute(tail, axis, [(i, (i + 1) % count) for i in range(ends)]),
                cells,
                lax.ppermute(head, axis, [((i + 1) % count, i) for i in range(ends)]),
            ],
            axis=dim,
        )
    return cells


def layer_norm(values):
    mean = jnp.mean(values, axis=-1, keepdims=True)
    centered = values - mean
    variance = jnp.mean(centered * centered, axis=-1, keepdims=True)
    return centered * lax.rsqrt(variance + 1e-05)


def pick_rows(table, indices):
    onehot = (indices[:, None] == jnp.arange(table.shape[0], dtype=jnp.int32)[None, :]).astype(
        jnp.bfloat16
    )
    return jnp.dot(onehot, table, preferred_element_type=jnp.float32).astype(jnp.bfloat16)


def edge_block(feats, sender_rows, receiver_rows, w_feat, w_out, count):
    base = jnp.einsum("ke,kd->ed", feats, w_feat, precision=lax.Precision.HIGHEST)
    pre = base + sender_rows.astype(jnp.float32) + receiver_rows.astype(jnp.float32)
    hidden = jax.nn.silu(pre).astype(jnp.bfloat16)
    out = layer_norm(jnp.dot(hidden, w_out, preferred_element_type=jnp.float32))
    live = (jnp.arange(feats.shape[1], dtype=jnp.int32) < count).astype(jnp.float32)
    return (out * live[:, None]).astype(jnp.bfloat16)


def aggregate(messages, receivers, nodes):
    onehot = (receivers[None, :] == jnp.arange(nodes, dtype=jnp.int32)[:, None]).astype(
        jnp.bfloat16
    )
    return jnp.dot(onehot, messages, preferred_element_type=jnp.float32).astype(jnp.bfloat16)


def node_block(latent, summed, w_in, w_out):
    joined = jnp.concatenate([latent, summed], axis=1)
    hidden = jax.nn.silu(jnp.dot(joined, w_in, preferred_element_type=jnp.float32)).astype(
        jnp.bfloat16
    )
    update = layer_norm(jnp.dot(hidden, w_out, preferred_element_type=jnp.float32))
    return (latent.astype(jnp.float32) + update).astype(jnp.bfloat16)


def body(
    grid_latent,
    mesh_latent,
    enc_feats,
    enc_sender,
    enc_receiver,
    enc_count,
    mesh_feats,
    mesh_sender,
    mesh_receiver,
    mesh_count,
    need_rows,
    w_enc_feat,
    w_enc_send,
    w_enc_recv,
    w_enc_out,
    w_enc_node_in,
    w_enc_node_out,
    w_proc_feat,
    w_proc_send,
    w_proc_recv,
    w_proc_out,
    w_proc_node_in,
    w_proc_node_out,
):
    nodes = mesh_latent.shape[0]
    width = mesh_latent.shape[1]
    blocks = lax.axis_size("tile")
    grid_proj = jnp.dot(grid_latent, w_enc_send, preferred_element_type=jnp.float32).astype(
        jnp.bfloat16
    )
    extended = padded(grid_proj, (("tile", 0),), HALO)
    sender_rows = pick_rows(extended, enc_sender)
    recv_proj = jnp.dot(mesh_latent, w_enc_recv, preferred_element_type=jnp.float32).astype(
        jnp.bfloat16
    )
    receiver_rows = pick_rows(recv_proj, enc_receiver)
    messages = edge_block(
        enc_feats, sender_rows, receiver_rows, w_enc_feat, w_enc_out, enc_count[0]
    )
    summed = aggregate(messages, enc_receiver, nodes)
    mesh_mid = node_block(mesh_latent, summed, w_enc_node_in, w_enc_node_out)
    send_proj = jnp.dot(mesh_mid, w_proc_send, preferred_element_type=jnp.float32).astype(
        jnp.bfloat16
    )
    wanted = need_rows[0]
    listed_per = wanted.shape[1]
    asked = lax.all_to_all(wanted, "tile", split_axis=0, concat_axis=0, tiled=True)
    outgoing = pick_rows(send_proj, asked.reshape(-1)).reshape(blocks, listed_per, width)
    listed = lax.all_to_all(outgoing, "tile", split_axis=0, concat_axis=0, tiled=True).reshape(
        blocks * listed_per, width
    )
    mesh_rows = pick_rows(listed, mesh_sender)
    proc_recv = jnp.dot(mesh_mid, w_proc_recv, preferred_element_type=jnp.float32).astype(
        jnp.bfloat16
    )
    proc_receiver_rows = pick_rows(proc_recv, mesh_receiver)
    proc_messages = edge_block(
        mesh_feats, mesh_rows, proc_receiver_rows, w_proc_feat, w_proc_out, mesh_count[0]
    )
    proc_summed = aggregate(proc_messages, mesh_receiver, nodes)
    return node_block(mesh_mid, proc_summed, w_proc_node_in, w_proc_node_out)


def solution(mesh):
    placed = (
        P(("groups", "tile"), None),
        P(("groups", "tile"), None),
        P(None, ("groups", "tile")),
        P(("groups", "tile")),
        P(("groups", "tile")),
        P(("groups", "tile")),
        P(None, ("groups", "tile")),
        P(("groups", "tile")),
        P(("groups", "tile")),
        P(("groups", "tile")),
        P(("groups", "tile"), None, None),
        P(),
        P(),
        P(),
        P(),
        P(),
        P(),
        P(),
        P(),
        P(),
        P(),
        P(),
        P(),
    )
    return jax.shard_map(
        body, mesh=mesh, in_specs=placed, out_specs=P(("groups", "tile"), None), check_vma=False
    )
```

profile of v0, /device:TPU:0, one launch (start us, length us, event | category | flops | bytes accessed | tf_op | source)
XLA Modules:
  0.0 76.6 jit_solution(9136991898325917282)
XLA Ops:
  0.0 1.2 %copy-done = bf16[1024,512]{1,0:T(8,128)(2,1)S(1)} copy-done((bf16[1024,512]{1,0:T(8,128)(2,1)S(1)}, bf16[1024,512]{1,0:T(8,128)(2,1)}, u32[]{:S(2)}) %copy-start) | copy-done | bytes 1048600
  1.2 1.7 %convolution_convert_fusion.3 = bf16[1024,512]{1,0:T(8,128)(2,1)S(1)} fusion(bf16[1024,512]{1,0:T(8,128)(2,1)S(1)} %copy-done, bf16[512,512]{1,0:T(8,128)(2,1)} %param.35), kind=kOutput, calls=%fused_computation.32 | convolution fusion | flops 537395200 | bytes 2621440 | tf_op jit(solution)/shard_map/dot_general | solution.py:93
  3.0 1.1 %copy-done.4 = bf16[1024,512]{1,0:T(8,128)(2,1)} copy-done((bf16[1024,512]{1,0:T(8,128)(2,1)}, bf16[1024,512]{1,0:T(8,128)(2,1)S(1)}, u32[]{:S(2)}) %copy-start.4) | copy-done | bytes 1048600
  4.0 0.8 %fusion.61 = (bf16[256,512]{1,0:T(8,128)(2,1)}, bf16[256,512]{1,0:T(8,128)(2,1)}) fusion(bf16[1024,512]{1,0:T(8,128)(2,1)S(1)} %convolution_convert_fusion.3), kind=kLoop, calls=%fused_computation.82 | loop fusion | bytes 1048576 | tf_op jit(solution)/shard_map/slice | solution.py:14
  4.8 3.1 %collective-permute-start = (bf16[256,512]{1,0:T(8,128)(2,1)}, bf16[256,512]{1,0:T(8,128)(2,1)}, u32[]{:S(2)}, u32[]{:S(2)}) collective-permute-start(bf16[256,512]{1,0:T(8,128)(2,1)} %get-tuple-element.5), channel_id=1, source_target_pairs={{0,1},{1,2},{2,3},{3,4},{4,5},{5,6},{6,7},{7,8},{8,9},{9,10},{10,1... | collective-permute-start | bytes 786440 | tf_op jit(solution)/shard_map/ppermute | solution.py:17
  7.9 1.3 %collective-permute-start.1 = (bf16[256,512]{1,0:T(8,128)(2,1)}, bf16[256,512]{1,0:T(8,128)(2,1)}, u32[]{:S(2)}, u32[]{:S(2)}) collective-permute-start(bf16[256,512]{1,0:T(8,128)(2,1)} %get-tuple-element.6), channel_id=1, source_target_pairs={{1,0},{2,1},{3,2},{4,3},{5,4},{6,5},{7,6},{8,7},{9,8},{10,9},{11,1... | collective-permute-start | bytes 786440 | tf_op jit(solution)/shard_map/ppermute | solution.py:19
  9.2 8.6 %all-to-all-start = ((s32[16,1,16]{2,1,0:T(1,128)}), s32[16,1,16]{2,1,0:T(1,128)S(1)}, u32[]{:S(2)}, u32[]{:S(2)}) async-start(s32[16,1,16]{2,1,0:T(1,128)} %bitcast.27), calls=%async_computation | async-start | bytes 16384 | tf_op jit(solution)/shard_map/all_to_all | solution.py:112
  18.5 6.2 %fusion.72 = f32[2048,512]{1,0:T(8,128)} fusion(f32[4,2048]{1,0:T(4,128)} %param.25, f32[4,512]{1,0:T(4,128)} %param.34), kind=kOutput, calls=%fused_computation.87 | convolution fusion | flops 50331648 | bytes 4235264 | tf_op jit(solution)/shard_map/ke,kd->ed/dot_general | solution.py:41
  24.6 2.0 %convolution_convert_fusion.2 = bf16[2048,512]{1,0:T(8,128)(2,1)S(1)} fusion(bf16[256,512]{1,0:T(8,128)(2,1)S(1)} %copy-done.2, bf16[512,512]{1,0:T(8,128)(2,1)} %param.36, s32[2048]{0:T(1024)S(1)} %copy-done.6), kind=kOutput, calls=%fused_computation.11 | convolution fusion | flops 672792576 | bytes 2891776 | tf_op jit(solution)/shard_map/dot_general | solution.py:37
  27.9 10.1 %fusion.62 = (f32[2048]{0:T(1024)S(1)}, f32[2048,512]{0,1:T(8,128)}) fusion(bf16[512,512]{1,0:T(8,128)(2,1)} %param.37, bf16[2048,512]{1,0:T(8,128)(2,1)S(1)} %convolution_convert_fusion.2, f32[2048,512]{1,0:T(8,128)} %fusion.72, s32[2048]{0:T(1024)S(1)} %copy-done.12, bf16[256,512]{1,0:T(8,128)(2,1)} %collective-permute-done.1, ...), kind=kOutput, calls=%fused_computation.83 | convolution fusion | flops 4314363904 | bytes 12599296 | tf_op jit(solution)/shard_map/dot_general | solution.py:44
  38.0 2.8 %multiply_reduce_fusion.1 = f32[2048]{0:T(1024)S(1)} fusion(f32[2048,512]{0,1:T(8,128)} %get-tuple-element.8, f32[2048]{0:T(1024)S(1)} %broadcast_multiply_fusion.1), kind=kLoop, calls=%fused_computation.7 | loop fusion | flops 3143680 | bytes 4210688 | tf_op jit(solution)/shard_map/reduce_sum | solution.py:29
  40.8 0.6 copy-done.1
  41.5 0.9 %fusion.23 = bf16[256,512]{1,0:T(8,128)(2,1)S(1)} fusion(f32[2048,512]{0,1:T(8,128)S(1)} %copy-done.1, f32[2048]{0:T(1024)S(1)} %fusion.50, f32[2048]{0:T(1024)S(1)} %add_rsqrt_fusion.1, f32[2048]{0:T(1024)S(1)} %broadcast_multiply_fusion.1, s32[2048]{0:T(1024)S(1)} %copy-done.6), kind=kOutput, calls=%fused_computation.34 | convolution fusion | flops 541720576 | bytes 4489216 | tf_op jit(solution)/shard_map/dot_general | solution.py:53
  42.4 1.8 %fusion.65 = (f32[256]{0:T(256)S(1)}, f32[256,512]{1,0:T(8,128)S(1)}) fusion(bf16[512,512]{1,0:T(8,128)(2,1)} %param.39, bf16[1024,512]{1,0:T(8,128)(2,1)S(1)} %copy-done.8, bf16[256,512]{1,0:T(8,128)(2,1)S(1)} %fusion.23, bf16[256,512]{1,0:T(8,128)(2,1)S(1)} %copy-done.2), kind=kOutput, calls=%fused_computation.84 | convolution fusion | flops 404487936 | bytes 2622464 | tf_op jit(solution)/shard_map/dot_general | solution.py:61
  44.9 2.3 %convolution_convert_fusion.5 = bf16[256,512]{1,0:T(8,128)(2,1)} fusion(bf16[256,512]{1,0:T(8,128)(2,1)S(1)} %add_convert_fusion.1, bf16[512,512]{1,0:T(8,128)(2,1)} %param.41, s32[256]{0:T(256)S(1)} %eq.108), kind=kOutput, calls=%fused_computation.36 | convolution fusion | flops 201654272 | bytes 1049600 | tf_op jit(solution)/shard_map/dot_general | solution.py:37
  47.1 6.1 %all-to-all-start.1 = ((bf16[16,16,512]{2,1,0:T(8,128)(2,1)}), bf16[16,16,512]{2,1,0:T(8,128)(2,1)}, u32[]{:S(2)}, u32[]{:S(2)}) async-start(bf16[16,16,512]{2,1,0:T(8,128)(2,1)} %bitcast.2), calls=%async_computation.1 | async-start | bytes 524288 | tf_op jit(solution)/shard_map/all_to_all | solution.py:114
  53.9 2.0 %convolution_convert_fusion = bf16[2048,512]{1,0:T(8,128)(2,1)S(1)} fusion(bf16[256,512]{1,0:T(8,128)(2,1)S(1)} %add_convert_fusion.1, bf16[512,512]{1,0:T(8,128)(2,1)} %param.42, s32[2048]{0:T(1024)S(1)} %copy-done.7), kind=kOutput, calls=%fused_computation.9 | convolution fusion | flops 672792576 | bytes 2891776 | tf_op jit(solution)/shard_map/dot_general | solution.py:37
  55.9 7.4 %all-to-all-done.1 = bf16[16,16,512]{2,1,0:T(8,128)(2,1)} async-done(((bf16[16,16,512]{2,1,0:T(8,128)(2,1)}), bf16[16,16,512]{2,1,0:T(8,128)(2,1)}, u32[]{:S(2)}, u32[]{:S(2)}) %all-to-all-start.1) | async-done | bytes 262176 | tf_op jit(solution)/shard_map/all_to_all | solution.py:114
  63.3 1.9 %convolution_convert_fusion.1 = bf16[2048,512]{1,0:T(8,128)(2,1)S(1)} fusion(bf16[256,512]{1,0:T(8,128)(2,1)} %bitcast.3, s32[2048]{0:T(1024)S(1)} %copy-done.5), kind=kOutput, calls=%fused_computation.10 | convolution fusion | flops 538443776 | bytes 2367488 | tf_op jit(solution)/shard_map/dot_general | solution.py:37
  65.3 4.9 %multiply_convert_fusion.1 = bf16[2048,512]{1,0:T(8,128)(2,1)S(1)} fusion(bf16[2048,512]{1,0:T(8,128)(2,1)S(1)} %convolution_convert_fusion, bf16[2048,512]{1,0:T(8,128)(2,1)S(1)} %convolution_convert_fusion.1, f32[4,2048]{1,0:T(4,128)S(1)} %copy-done.11, f32[4,512]{1,0:T(4,128)S(1)} %copy-done.13), kind=kOutput, calls=%fused_computation.5 | convolution fusion | flops 59768832 | bytes 6332416 | tf_op jit(solution)/shard_map/ke,kd->ed/dot_general | solution.py:41
  70.2 1.3 %fusion.68 = (f32[2048]{0:T(1024)S(1)}, f32[2048,512]{0,1:T(8,128)S(1)}) fusion(bf16[2048,512]{1,0:T(8,128)(2,1)S(1)} %multiply_convert_fusion.1, bf16[512,512]{1,0:T(8,128)(2,1)S(1)} %copy-done.3), kind=kOutput, calls=%fused_computation.85 | convolution fusion | flops 1074788352 | bytes 6823936 | tf_op jit(solution)/shard_map/dot_general | solution.py:44
  72.1 1.6 %fusion.22 = bf16[256,512]{1,0:T(8,128)(2,1)} fusion(f32[2048,512]{0,1:T(8,128)S(1)} %get-tuple-element.12, f32[2048]{0:T(1024)S(1)} %fusion.51, f32[2048]{0:T(1024)S(1)} %add_rsqrt_fusion, f32[2048]{0:T(1024)S(1)} %broadcast_multiply_fusion, s32[2048]{0:T(1024)S(1)} %copy-done.7), kind=kOutput, calls=%fused_computation.33 | convolution fusion | flops 541720576 | bytes 4489216 | tf_op jit(solution)/shard_map/dot_general | solution.py:53
  73.7 1.7 %fusion.69 = (f32[256]{0:T(256)S(1)}, f32[256,512]{1,0:T(8,128)S(1)}) fusion(bf16[512,512]{1,0:T(8,128)(2,1)S(1)} %copy-done.10, bf16[1024,512]{1,0:T(8,128)(2,1)S(1)} %copy-done.9, bf16[256,512]{1,0:T(8,128)(2,1)} %fusion.22, bf16[256,512]{1,0:T(8,128)(2,1)S(1)} %add_convert_fusion.1), kind=kOutput, calls=%fused_computation.86 | convolution fusion | flops 404487936 | bytes 2622464 | tf_op jit(solution)/shard_map/dot_general | solution.py:61
  75.7 0.9 %add_convert_fusion = bf16[256,512]{1,0:T(8,128)(2,1)} fusion(bf16[256,512]{1,0:T(8,128)(2,1)S(1)} %add_convert_fusion.1, f32[256,512]{1,0:T(8,128)S(1)} %get-tuple-element.14, f32[256]{0:T(256)S(1)} %add_rsqrt_fusion.2, f32[256]{0:T(256)S(1)} %broadcast_multiply_fusion.2), kind=kLoop, calls=%fused_computation.52 | loop fusion | flops 655360 | bytes 1050624 | tf_op jit(solution)/shard_map/convert_element_type | solution.py:62
  (45 shorter events, 2.4 us)
Async XLA Ops:
  0.0 1.2 %copy-start = (bf16[1024,512]{1,0:T(8,128)(2,1)S(1)}, bf16[1024,512]{1,0:T(8,128)(2,1)}, u32[]{:S(2)}) copy-start(bf16[1024,512]{1,0:T(8,128)(2,1)} %param.23) | copy-start | bytes 3145732
  0.0 24.6 %copy-start.2 = (bf16[256,512]{1,0:T(8,128)(2,1)S(1)}, bf16[256,512]{1,0:T(8,128)(2,1)}, u32[]{:S(2)}) copy-start(bf16[256,512]{1,0:T(8,128)(2,1)} %param.24) | copy-start | bytes 786436
  0.0 24.6 %copy-start.6 = (s32[2048]{0:T(1024)S(1)}, s32[2048]{0:T(1024)}, u32[]{:S(2)}) copy-start(s32[2048]{0:T(1024)} %param.27) | copy-start | bytes 24580
  3.0 1.1 %copy-start.4 = (bf16[1024,512]{1,0:T(8,128)(2,1)}, bf16[1024,512]{1,0:T(8,128)(2,1)S(1)}, u32[]{:S(2)}) copy-start(bf16[1024,512]{1,0:T(8,128)(2,1)S(1)} %convolution_convert_fusion.3) | copy-start | bytes 3145732
  4.0 23.9 %copy-start.12 = (s32[2048]{0:T(1024)S(1)}, s32[2048]{0:T(1024)}, u32[]{:S(2)}) copy-start(s32[2048]{0:T(1024)} %param.26) | copy-start | bytes 24580
  4.8 23.1 %collective-permute-start = (bf16[256,512]{1,0:T(8,128)(2,1)}, bf16[256,512]{1,0:T(8,128)(2,1)}, u32[]{:S(2)}, u32[]{:S(2)}) collective-permute-start(bf16[256,512]{1,0:T(8,128)(2,1)} %get-tuple-element.5), channel_id=1, source_target_pairs={{0,1},{1,2},{2,3},{3,4},{4,5},{5,6},{6,7},{7,8},{8,9},{9,10},{10,1... | collective-permute-start | bytes 786440 | tf_op jit(solution)/shard_map/ppermute | solution.py:17
  7.9 20.0 %collective-permute-start.1 = (bf16[256,512]{1,0:T(8,128)(2,1)}, bf16[256,512]{1,0:T(8,128)(2,1)}, u32[]{:S(2)}, u32[]{:S(2)}) collective-permute-start(bf16[256,512]{1,0:T(8,128)(2,1)} %get-tuple-element.6), channel_id=1, source_target_pairs={{1,0},{2,1},{3,2},{4,3},{5,4},{6,5},{7,6},{8,7},{9,8},{10,9},{11,1... | collective-permute-start | bytes 786440 | tf_op jit(solution)/shard_map/ppermute | solution.py:19
  9.2 17.5 %all-to-all-start = ((s32[16,1,16]{2,1,0:T(1,128)}), s32[16,1,16]{2,1,0:T(1,128)S(1)}, u32[]{:S(2)}, u32[]{:S(2)}) async-start(s32[16,1,16]{2,1,0:T(1,128)} %bitcast.27), calls=%async_computation | async-start | bytes 16384 | tf_op jit(solution)/shard_map/all_to_all | solution.py:112
  38.0 3.4 %copy-start.1 = (f32[2048,512]{0,1:T(8,128)S(1)}, f32[2048,512]{0,1:T(8,128)}, u32[]{:S(2)}) copy-start(f32[2048,512]{0,1:T(8,128)} %get-tuple-element.8) | copy-start | bytes 12582916
  38.0 4.4 %copy-start.8 = (bf16[1024,512]{1,0:T(8,128)(2,1)S(1)}, bf16[1024,512]{1,0:T(8,128)(2,1)}, u32[]{:S(2)}) copy-start(bf16[1024,512]{1,0:T(8,128)(2,1)} %param.38) | copy-start | bytes 3145732
  42.4 11.5 %copy-start.7 = (s32[2048]{0:T(1024)S(1)}, s32[2048]{0:T(1024)}, u32[]{:S(2)}) copy-start(s32[2048]{0:T(1024)} %param.31) | copy-start | bytes 24580
  44.3 19.0 %copy-start.5 = (s32[2048]{0:T(1024)S(1)}, s32[2048]{0:T(1024)}, u32[]{:S(2)}) copy-start(s32[2048]{0:T(1024)} %param.30) | copy-start | bytes 24580
  44.7 20.6 %copy-start.11 = (f32[4,2048]{1,0:T(4,128)S(1)}, f32[4,2048]{1,0:T(4,128)}, u32[]{:S(2)}) copy-start(f32[4,2048]{1,0:T(4,128)} %param.29) | copy-start | bytes 98308
  44.9 20.4 %copy-start.13 = (f32[4,512]{1,0:T(4,128)S(1)}, f32[4,512]{1,0:T(4,128)}, u32[]{:S(2)}) copy-start(f32[4,512]{1,0:T(4,128)} %param.40) | copy-start | bytes 24580
  47.1 16.2 %all-to-all-start.1 = ((bf16[16,16,512]{2,1,0:T(8,128)(2,1)}), bf16[16,16,512]{2,1,0:T(8,128)(2,1)}, u32[]{:S(2)}, u32[]{:S(2)}) async-start(bf16[16,16,512]{2,1,0:T(8,128)(2,1)} %bitcast.2), calls=%async_computation.1 | async-start | bytes 524288 | tf_op jit(solution)/shard_map/all_to_all | solution.py:114
  65.3 4.9 %copy-start.3 = (bf16[512,512]{1,0:T(8,128)(2,1)S(1)}, bf16[512,512]{1,0:T(8,128)(2,1)}, u32[]{:S(2)}) copy-start(bf16[512,512]{1,0:T(8,128)(2,1)} %param.43) | copy-start | bytes 1572868
  71.5 2.2 %copy-start.9 = (bf16[1024,512]{1,0:T(8,128)(2,1)S(1)}, bf16[1024,512]{1,0:T(8,128)(2,1)}, u32[]{:S(2)}) copy-start(bf16[1024,512]{1,0:T(8,128)(2,1)} %param.44) | copy-start | bytes 3145732
  71.5 2.2 %copy-start.10 = (bf16[512,512]{1,0:T(8,128)(2,1)S(1)}, bf16[512,512]{1,0:T(8,128)(2,1)}, u32[]{:S(2)}) copy-start(bf16[512,512]{1,0:T(8,128)(2,1)} %param.45) | copy-start | bytes 1572868
where the time goes:
time: 77.2 us; the launch traced here: 76.6 us
  matrix products  38.6 us (50%)
  starting transfers between devices  19 us (25%)
  waiting for transfers between devices  7.4 us (10%)
  other arithmetic  5.4 us (7%)
  local copies, waits for them, and re-layouts  4.38 us (6%)
  between operations  1.76 us (2%)
    dot_general x2, matrix products, edge_block(): out = layer_norm(jnp.dot(hidden, w_out, preferred_element_type=jnp.float32))  11.4 us
    dot_general x2, matrix products, edge_block(): jnp.einsum('ke,kd->ed', feats, w_feat, precision=lax.Precision.HIGHEST)  11 us
    all_to_all x1, starting transfers between devices, body(): lax.all_to_all(wanted, 'tile', split_axis=0, concat_axis=0, tiled=True)  8.61 us
    dot_general x4, matrix products, pick_rows(): jnp.dot(onehot, table, preferred_element_type=jnp.float32)  8.27 us
    all_to_all x1, waiting for transfers between devices, body(): lax.all_to_all(outgoing, 'tile', split_axis=0, concat_axis=0, tiled=True)  7.39 us
    all_to_all x1, starting transfers between devices, body(): lax.all_to_all(outgoing, 'tile', split_axis=0, concat_axis=0, tiled=True)  6.06 us
    reduce_sum x4, other arithmetic, layer_norm(): variance = jnp.mean(centered * centered, axis=-1, keepdims=True)  3.72 us
    dot_general x2, matrix products, node_block(): jnp.dot(hidden, w_out, preferred_element_type=jnp.float32)  3.58 us
  transfers between devices with their start and end apart: 4, of which 1 were waited for; matrix products, arithmetic and copies ran while one was open for 15% of the time, Pallas kernels for 0%

commit v1 on v0

v1 whole, which is shorter than its diff:
```python
import functools

import jax
import jax.numpy as jnp
from jax import lax
from jax.experimental import pallas as pl
from jax.experimental.pallas import tpu as pltpu
from jax.sharding import PartitionSpec as P

HALO = 256
BLOCK = 512
F32, BF16 = jnp.float32, jnp.bfloat16
NN = (((1,), (0,)), ((), ()))
NT = (((1,), (1,)), ((), ()))
TN = (((0,), (0,)), ((), ()))
TT = (((0,), (1,)), ((), ()))


def mul(a, b, dims=NN):
    return lax.dot_general(a, b, dims, preferred_element_type=F32)


def swish(v):
    half = 0.5 * v
    return half * jnp.tanh(half) + half


def norm(x, axis):
    size = x.shape[axis]
    centered = x - jnp.sum(x, axis=axis, keepdims=True) * (1.0 / size)
    variance = jnp.sum(centered * centered, axis=axis, keepdims=True) * (1.0 / size)
    return centered, lax.rsqrt(variance + 1e-05)


def places(rows, indices):
    at = lax.broadcasted_iota(jnp.int32, (rows, indices.shape[1]), 0).astype(jnp.int16)
    one, zero = jnp.array(1, BF16), jnp.array(0, BF16)
    return jnp.where(at == indices.astype(jnp.int16), one, zero)


def split(x):
    high = x.astype(BF16)
    return high, (x - high.astype(F32)).astype(BF16)


def stack_feats(feats, w_feat, fa, wa):
    rows = feats.shape[0]
    fa[...] = jnp.zeros(fa.shape, F32)
    wa[...] = jnp.zeros(wa.shape, F32)
    f_high, f_low = split(feats[...])
    w_high, w_low = split(w_feat[...])
    for at, (f, w) in enumerate(((f_high, w_high), (f_high, w_low), (f_low, w_high))):
        fa[at * rows : (at + 1) * rows, :] = f.astype(F32)
        wa[at * rows : (at + 1) * rows, :] = w.astype(F32)


def fetch(pairs, sems):
    copies = [pltpu.make_async_copy(a, b, sems.at[i]) for i, (a, b) in enumerate(pairs)]
    for copy in copies:
        copy.start()

    def ready(*which):
        for i in which:
            copies[i].wait()

    return ready


def summed_messages(total, pre_of, to_of, w_out, count):
    w_out = w_out[...]
    held = {}

    def first(i):
        return to_of(i), swish(pre_of(i)).astype(BF16)

    def second(i, to, hidden):
        return to, mul(w_out, hidden, TN)

    def third(i, to, out):
        out, scale = norm(out, 0)
        live = lax.broadcasted_iota(jnp.int32, (1, BLOCK), 1) + i * BLOCK < count
        return to, (out * jnp.where(live, scale, 0.0)).astype(BF16)

    def last(i, to, message):
        return (mul(to, message, NT),)

    stages = (first, second, third, last)
    summed = None
    for step in range(total // BLOCK + len(stages) - 1):
        for at, stage in enumerate(stages):
            i = step - at
            if 0 <= i < total // BLOCK:
                held[i] = stage(i, *held.get(i, ()))
                if stage is last:
                    part = held.pop(i)[0]
                    summed = part if summed is None else summed + part
    return summed.astype(BF16)


def nodes_of(latent, summed, w_in, w_out):
    width = latent.shape[1]
    hidden = swish(mul(latent, w_in[:width, :]) + mul(summed, w_in[width:, :])).astype(BF16)
    centered, scale = norm(mul(hidden, w_out[...]), 1)
    return (latent.astype(F32) + centered * scale).astype(BF16)


def in_a_row(asked, rows):
    blocks, _, per = asked.shape
    for i in range(blocks):
        rows[i : i + 1, :] = asked[i].astype(F32)
    size = (per, blocks * per)
    column = lax.broadcasted_iota(jnp.int32, size, 1) % per
    repeat = (column == lax.broadcasted_iota(jnp.int32, size, 0)).astype(F32).astype(BF16)
    wide = mul(rows[...].astype(BF16), repeat)
    size = wide.shape
    block = lax.broadcasted_iota(jnp.int32, size, 1) // per
    own = block == lax.broadcasted_iota(jnp.int32, size, 0)
    return jnp.sum(jnp.where(own, wide, 0.0), axis=0, keepdims=True).astype(jnp.int32)


def band_ends(grid_any, pair_any, other_any, pair, other, sems, out_sems):
    first = (lax.axis_index("tile") % 2) * (grid_any.shape[0] - HALO)
    last = grid_any.shape[0] - HALO - first
    fetch(
        (
            (grid_any.at[pl.ds(pl.multiple_of(last, HALO), HALO), :], pair),
            (grid_any.at[pl.ds(pl.multiple_of(first, HALO), HALO), :], other),
        ),
        sems,
    )(0, 1)
    fetch(((pair, pair_any), (other, other_any)), out_sems)(0, 1)


def encode(
    from_pair, from_other,
    count_any, feats_any, sender_any, receiver_any, feat_any, latent_any, recv_any, send_any,
    grid_any, out_any, in_any, node_any, next_any,
    mid, sent,
    count, feats, sender, receiver, w_feat, latent, w_recv, w_send, grid, w_out, w_in, w_node,
    w_next, table, recv_table, fa, wa, sems,
):
    ready = fetch(
        (
            (feats_any, feats), (feat_any, w_feat), (latent_any, latent), (recv_any, w_recv),
            (send_any, w_send), (grid_any, grid), (sender_any, sender), (receiver_any, receiver),
            (out_any, w_out), (count_any, count), (in_any, w_in), (node_any, w_node),
            (next_any, w_next),
        ),
        sems,
    )
    own = grid.shape[0]
    ready(0, 1)
    stack_feats(feats, w_feat, fa, wa)
    ready(2, 3)
    recv_table[...] = mul(w_recv[...], latent[...], TT).astype(BF16)
    ready(4)
    table[:, :HALO] = mul(w_send[...], from_pair[...], TT).astype(BF16)
    table[:, HALO : 2 * HALO] = mul(w_send[...], from_other[...], TT).astype(BF16)
    ready(5)
    table[:, 2 * HALO :] = mul(w_send[...], grid[...], TT).astype(BF16)
    wab = wa[...].astype(BF16)
    ready(6, 7, 8, 9)
    odd = lax.axis_index("tile") % 2
    above, below = (1 - odd) * HALO, odd * HALO

    def to_of(i):
        return places(recv_table.shape[1], receiver[:, pl.ds(i * BLOCK, BLOCK)])

    def pre_of(i):
        span = pl.ds(i * BLOCK, BLOCK)
        s = sender[:, span]
        s = jnp.where(
            s < HALO,
            s + above,
            jnp.where(s < HALO + own, s + HALO, s - (HALO + own) + below),
        )
        pre = mul(table[...], places(table.shape[1], s))
        pre += mul(recv_table[...], to_of(i))
        return pre + mul(wab, fa[:, span].astype(BF16), TN)

    summed = summed_messages(sender.shape[1], pre_of, to_of, w_out, count[0])
    ready(10, 11, 12)
    middle = nodes_of(latent[...], summed, w_in, w_node)
    mid[...] = middle
    sent[...] = mul(middle, w_next[...]).astype(BF16)


def answer(sent, asked, outgoing_any, outgoing, rows, sems):
    at = places(sent.shape[0], in_a_row(asked, rows))
    outgoing[...] = mul(at, sent[...], TN).astype(BF16)
    fetch(((outgoing, outgoing_any),), sems)(0)


def process_own(
    mid, feats_any, receiver_any, feat_any, recv_any, pre,
    feats, receiver, w_feat, w_recv, recv_table, fa, wa, sems,
):
    ready = fetch(
        (
            (feats_any, feats), (feat_any, w_feat), (recv_any, w_recv), (receiver_any, receiver),
        ),
        sems,
    )
    ready(0, 1)
    stack_feats(feats, w_feat, fa, wa)
    ready(2)
    recv_table[...] = mul(w_recv[...], mid[...], TT).astype(BF16)
    wab = wa[...].astype(BF16)
    ready(3)
    for start in range(0, pre.shape[1], BLOCK):
        span = pl.ds(start, BLOCK)
        part = mul(recv_table[...], places(recv_table.shape[1], receiver[:, span]))
        pre[:, span] = (part + mul(wab, fa[:, span].astype(BF16), TN)).astype(pre.dtype)


def process_rest(
    mid, pre, listed, count_any, sender_any, receiver_any, out_any, in_any, node_any,
    result_any,
    count, sender, receiver, w_out, w_in, w_node, result, sems, out_sems,
):
    ready = fetch(
        (
            (sender_any, sender), (receiver_any, receiver), (count_any, count), (out_any, w_out),
            (in_any, w_in), (node_any, w_node),
        ),
        sems,
    )
    table = listed[...].T
    ready(0, 1, 2, 3)

    def to_of(i):
        return places(mid.shape[0], receiver[:, pl.ds(i * BLOCK, BLOCK)])

    def pre_of(i):
        span = pl.ds(i * BLOCK, BLOCK)
        return pre[:, span] + mul(table, places(table.shape[1], sender[:, span]))

    summed = summed_messages(sender.shape[1], pre_of, to_of, w_out, count[0])
    ready(4, 5)
    result[...] = nodes_of(mid[...], summed, w_in, w_node)
    fetch(((result, result_any),), out_sems)(0)


S, V, H = (pl.BlockSpec(memory_space=m) for m in (pltpu.SMEM, pltpu.VMEM, pltpu.HBM))
ONE = "one integer"


def shape(*sizes, dtype=BF16):
    return jax.ShapeDtypeStruct(sizes, dtype)


def call(kernel, name, near, far, near_outs, far_outs, scratch, copies):
    return pl.pallas_call(
        kernel,
        out_shape=near_outs + far_outs,
        in_specs=[V] * len(near) + [H] * len(far),
        out_specs=[V] * len(near_outs) + [H] * len(far_outs),
        scratch_shapes=[
            pltpu.SMEM((1,), jnp.int32) if s is ONE else pltpu.VMEM(s.shape, s.dtype)
            for s in scratch
        ]
        + [pltpu.SemaphoreType.DMA((n,)) for n in copies],
        compiler_params=pltpu.CompilerParams(vmem_limit_bytes=48 * 2**20),
        name=name,
    )(*near, *(x if x.size == 1 else pltpu.with_memory_space_constraint(x, pltpu.HBM) for x in far))


def body(
    grid_latent, mesh_latent, enc_feats, enc_sender, enc_receiver, enc_count,
    mesh_feats, mesh_sender, mesh_receiver, mesh_count, need_rows,
    w_enc_feat, w_enc_send, w_enc_recv, w_enc_out, w_enc_node_in, w_enc_node_out,
    w_proc_feat, w_proc_send, w_proc_recv, w_proc_out, w_proc_node_in, w_proc_node_out,
):
    nodes, width = mesh_latent.shape
    rows = grid_latent.shape[0]
    slots = enc_feats.shape[1]
    blocks = lax.axis_size("tile")
    per = need_rows.shape[2]
    square = shape(width, width)
    node_rows = shape(nodes, width)
    edge_index = shape(1, slots, dtype=jnp.int32)
    edge_feats = shape(*enc_feats.shape, dtype=F32)
    feat_weight = shape(*w_enc_feat.shape, dtype=F32)
    stacked = [shape(16, slots, dtype=F32), shape(16, width, dtype=F32)]
    enc_sender, enc_receiver, mesh_sender, mesh_receiver = (
        x.reshape(1, slots) for x in (enc_sender, enc_receiver, mesh_sender, mesh_receiver)
    )

    asked = lax.all_to_all(
        need_rows.reshape(blocks, 1, per), "tile", split_axis=0, concat_axis=0, tiled=True
    )
    for_pair, for_other = call(
        band_ends, "band_ends", [], [grid_latent], [], [shape(HALO, width)] * 2,
        [shape(HALO, width)] * 2, (2, 2),
    )
    pairs = [(i, i ^ 1) for i in range(blocks)]
    others = [(i, i + 1 if i % 2 else i - 1) for i in range(1, blocks - 1)]
    from_pair = lax.ppermute(for_pair, "tile", pairs)
    from_other = lax.ppermute(for_other, "tile", others)
    mid, sent = call(
        encode,
        "encode",
        [from_pair, from_other],
        [
            enc_count, enc_feats, enc_sender, enc_receiver, w_enc_feat, mesh_latent, w_enc_recv,
            w_enc_send, grid_latent, w_enc_out, w_enc_node_in, w_enc_node_out, w_proc_send,
        ],
        [node_rows, node_rows],
        [],
        [
            ONE, edge_feats, edge_index, edge_index, feat_weight, node_rows, square, square,
            shape(rows, width), square, shape(2 * width, width), square, square,
            shape(width, rows + 2 * HALO), shape(width, nodes),
        ]
        + stacked,
        (13,),
    )
    (outgoing,) = call(
        answer,
        "answer",
        [sent, asked],
        [],
        [],
        [shape(blocks * per, width)],
        [shape(blocks * per, width), shape(blocks, per, dtype=F32)],
        (1,),
    )
    listed = lax.all_to_all(
        outgoing.reshape(blocks, per, width), "tile", split_axis=0, concat_axis=0, tiled=True
    ).reshape(blocks * per, width)
    (pre,) = call(
        process_own,
        "process_own",
        [mid],
        [mesh_feats, mesh_receiver, w_proc_feat, w_proc_recv],
        [shape(width, slots)],
        [],
        [edge_feats, edge_index, feat_weight, square, shape(width, nodes)] + stacked,
        (4,),
    )
    (result,) = call(
        process_rest,
        "process_rest",
        [mid, pre, listed],
        [
            mesh_count, mesh_sender, mesh_receiver, w_proc_out, w_proc_node_in, w_proc_node_out,
        ],
        [],
        [node_rows],
        [
            ONE, edge_index, edge_index, square, shape(2 * width, width), square, node_rows,
        ],
        (6, 1),
    )
    return result


def solution(mesh):
    split_rows = P(("groups", "tile"), None)
    split_columns = P(None, ("groups", "tile"))
    split_flat = P(("groups", "tile"))
    placed = (
        split_rows, split_rows, split_columns, split_flat, split_flat, split_flat,
        split_columns, split_flat, split_flat, split_flat,
        P(("groups", "tile"), None, None),
    ) + (P(),) * 12
    return jax.shard_map(
        body, mesh=mesh, in_specs=placed, out_specs=split_rows, check_vma=False
    )
```

time: 77.2 us -> 47.5 us (0.62)
  matrix products: 38.6 us -> 0 us
  Pallas kernels: 0 us -> 22.2 us
  other arithmetic: 5.4 us -> 0 us
  local copies, waits for them, and re-layouts: 4.38 us -> 0 us
  starting transfers between devices: 19 us -> 16.7 us
    dot_general x13 -> x0, matrix products: 38.6 us -> none  [the longest x2 11.4 us: edge_block(): out = layer_norm(jnp.dot(hidden, w_out, preferred_element_type=jnp.float32))]
    pallas_call x0 -> x5, Pallas kernels: none -> 22.2 us  [call(): pl.pallas_call(kernel, out_shape=near_outs + far_outs, in_specs=[V] * len...]
    reduce_sum x4 -> x0, other arithmetic: 3.72 us -> none  [layer_norm(): variance = jnp.mean(centered * centered, axis=-1, keepdims=True)]
    ppermute x2, starting transfers between devices: 4.35 us -> 1.18 us  [the longest x1 0.67 us: body(): from_other = lax.ppermute(for_other, 'tile', others)]
    unnamed x28 -> x0, local copies, waits for them, and re-layouts: 2.98 us -> none
    convert_element_type x4 -> x0, other arithmetic: 1.04 us -> none  [the longest x2 1.03 us: node_block(): return (latent.astype(jnp.float32) + update).astype(jnp.bfloat16)]
    all_to_all x2, starting transfers between devices: 14.7 us -> 15.5 us  [the longest x1 8.8 us: body(): lax.all_to_all(need_rows.reshape(blocks, 1, per), 'tile', split_axis=0, c...]
    slice x1 -> x0, local copies, waits for them, and re-layouts: 0.81 us -> none  [padded(): lax.slice_in_dim(cells, cells.shape[dim] - width, cells.shape[dim], axis=...]
  transfers between devices with their start and end apart: 4 -> 4, of which waited for: 1 -> 1; matrix products, arithmetic and copies ran while one was open for 15% -> 0% of each run, Pallas kernels for 0% -> 30%
where the time goes in v1:
time: 47.5 us; the launch traced here: 47.1 us
  Pallas kernels  22.2 us (47%)
  starting transfers between devices  16.7 us (35%)
  waiting for transfers between devices  6.71 us (14%)
  between operations  1.54 us (3%)
    pallas_call x5, Pallas kernels, call(): pl.pallas_call(kernel, out_shape=near_outs + far_outs, in_specs=[V] * len...  22.2 us
    all_to_all x1, starting transfers between devices, body(): lax.all_to_all(need_rows.reshape(blocks, 1, per), 'tile', split_axis=0, c...  8.8 us
    all_to_all x1, starting transfers between devices, body(): lax.all_to_all(outgoing.reshape(blocks, per, width), 'tile', split_axis=0...  6.75 us
    all_to_all x1, waiting for transfers between devices, body(): lax.all_to_all(outgoing.reshape(blocks, per, width), 'tile', split_axis=0...  6.7 us
  transfers between devices with their start and end apart: 4, of which 1 were waited for; matrix products, arithmetic and copies ran while one was open for 0% of the time, Pallas kernels for 30%

profile of v1, /device:TPU:0, one launch (start us, length us, event | category | flops | bytes accessed | tf_op | source)
XLA Modules:
  0.0 47.1 jit_solution(12757281637408043730)
XLA Ops:
  0.0 1.1 %band_ends.1 = (bf16[256,512]{1,0:T(8,128)(2,1)S(1)}, bf16[256,512]{1,0:T(8,128)(2,1)S(1)}) custom-call(bf16[1024,512]{1,0:T(8,128)(2,1)} %grid_any.3), custom_call_target="tpu_custom_call" | custom-call | tf_op jit(solution)/shard_map/band_ends/pallas_call | solution.py:253
  1.1 0.5 %collective-permute-start = (bf16[256,512]{1,0:T(8,128)(2,1)S(1)}, bf16[256,512]{1,0:T(8,128)(2,1)S(1)}, u32[]{:S(2)}, u32[]{:S(2)}) collective-permute-start(bf16[256,512]{1,0:T(8,128)(2,1)S(1)} %get-tuple-element.9), channel_id=1, source_target_pairs={{0,1},{1,0},{2,3},{3,2},{4,5},{5,4},{6,7},{7,6},{8,9},{9,8},{10,11... | collective-permute-start | bytes 786440 | tf_op jit(solution)/shard_map/ppermute | solution.py:298
  1.6 0.7 %collective-permute-start.1 = (bf16[256,512]{1,0:T(8,128)(2,1)S(1)}, bf16[256,512]{1,0:T(8,128)(2,1)S(1)}, u32[]{:S(2)}, u32[]{:S(2)}) collective-permute-start(bf16[256,512]{1,0:T(8,128)(2,1)S(1)} %get-tuple-element.10), channel_id=1, source_target_pairs={{1,2},{2,1},{3,4},{4,3},{5,6},{6,5},{7,8},{8,7},{9,10},{10,9},{11,... | collective-permute-start | bytes 786440 | tf_op jit(solution)/shard_map/ppermute | solution.py:299
  2.3 8.8 %all-to-all-start = ((s32[16,1,16]{2,1,0:T(1,128)}), s32[16,1,16]{2,1,0:T(1,128)S(1)}, u32[]{:S(2)}, u32[]{:S(2)}) async-start(s32[16,1,16]{2,1,0:T(1,128)} %bitcast.13), calls=%async_computation | async-start | bytes 16384 | tf_op jit(solution)/shard_map/all_to_all | solution.py:289
  11.8 0.0 collective-permute-done.from_pair
  11.8 0.0 collective-permute-done.1.from_other
  11.8 11.4 %encode.1 = (bf16[256,512]{1,0:T(8,128)(2,1)S(1)}, bf16[256,512]{1,0:T(8,128)(2,1)S(1)}) custom-call(bf16[256,512]{1,0:T(8,128)(2,1)S(1)} %collective-permute-done.from_pair, bf16[256,512]{1,0:T(8,128)(2,1)S(1)} %collective-permute-done.1.from_other, s32[1]{0:T(128)S(6)} %copy.24.count_any, f32[4,2048]{1,0:T(4,128)} %feats_any.2, s32[1,2048]{1,0:T(1,128)} %bitcast.10, ...), custom_call_target="tpu_custom_call" | custom-call | tf_op jit(solution)/shard_map/encode/pallas_call | solution.py:253
  23.2 0.0 all-to-all-done.asked
  23.2 1.1 %answer.1 = bf16[256,512]{1,0:T(8,128)(2,1)} custom-call(bf16[256,512]{1,0:T(8,128)(2,1)S(1)} %get-tuple-element.12.sent, s32[16,1,16]{2,1,0:T(1,128)S(1)} %all-to-all-done.asked), custom_call_target="tpu_custom_call" | custom-call | tf_op jit(solution)/shard_map/answer/pallas_call | solution.py:253
  24.3 6.7 %all-to-all-start.1 = ((bf16[16,16,512]{2,1,0:T(8,128)(2,1)}), bf16[16,16,512]{2,1,0:T(8,128)(2,1)S(1)}, u32[]{:S(2)}, u32[]{:S(2)}) async-start(bf16[16,16,512]{2,1,0:T(8,128)(2,1)} %bitcast.4), calls=%async_computation.1 | async-start | bytes 524288 | tf_op jit(solution)/shard_map/all_to_all | solution.py:328
  31.7 2.7 %process_own.1.pre = bf16[512,2048]{1,0:T(8,128)(2,1)S(1)} custom-call(bf16[256,512]{1,0:T(8,128)(2,1)S(1)} %get-tuple-element.11.mid, f32[4,2048]{1,0:T(4,128)} %feats_any.3, s32[1,2048]{1,0:T(1,128)} %bitcast.8, f32[4,512]{1,0:T(4,128)} %feat_any.3, bf16[512,512]{1,0:T(8,128)(2,1)} %recv_any.3), custom_call_target="tpu_custom_call" | custom-call | tf_op jit(solution)/shard_map/process_own/pallas_call | solution.py:253
  34.4 6.7 %all-to-all-done.1 = bf16[16,16,512]{2,1,0:T(8,128)(2,1)S(1)} async-done(((bf16[16,16,512]{2,1,0:T(8,128)(2,1)}), bf16[16,16,512]{2,1,0:T(8,128)(2,1)S(1)}, u32[]{:S(2)}, u32[]{:S(2)}) %all-to-all-start.1) | async-done | bytes 262176 | tf_op jit(solution)/shard_map/all_to_all | solution.py:328
  41.1 5.9 %process_rest.1 = bf16[256,512]{1,0:T(8,128)(2,1)} custom-call(bf16[256,512]{1,0:T(8,128)(2,1)S(1)} %get-tuple-element.11.mid, bf16[512,2048]{1,0:T(8,128)(2,1)S(1)} %process_own.1.pre, bf16[256,512]{1,0:T(8,128)(2,1)S(1)} %bitcast.7, s32[1]{0:T(128)S(6)} %copy.25.count_any, s32[1,2048]{1,0:T(1,128)} %bitcast.12, s32[1,2048]{1,0:T(1,128)} %bitcast.9, ...), custom_call_target="tpu_custom_call" | custom-call | tf_op jit(solution)/shard_map/process_rest/pallas_call | solution.py:253
Async XLA Ops:
  1.1 10.6 %collective-permute-start = (bf16[256,512]{1,0:T(8,128)(2,1)S(1)}, bf16[256,512]{1,0:T(8,128)(2,1)S(1)}, u32[]{:S(2)}, u32[]{:S(2)}) collective-permute-start(bf16[256,512]{1,0:T(8,128)(2,1)S(1)} %get-tuple-element.9), channel_id=1, source_target_pairs={{0,1},{1,0},{2,3},{3,2},{4,5},{5,4},{6,7},{7,6},{8,9},{9,8},{10,11... | collective-permute-start | bytes 786440 | tf_op jit(solution)/shard_map/ppermute | solution.py:298
  1.6 10.1 %collective-permute-start.1 = (bf16[256,512]{1,0:T(8,128)(2,1)S(1)}, bf16[256,512]{1,0:T(8,128)(2,1)S(1)}, u32[]{:S(2)}, u32[]{:S(2)}) collective-permute-start(bf16[256,512]{1,0:T(8,128)(2,1)S(1)} %get-tuple-element.10), channel_id=1, source_target_pairs={{1,2},{2,1},{3,4},{4,3},{5,6},{6,5},{7,8},{8,7},{9,10},{10,9},{11,... | collective-permute-start | bytes 786440 | tf_op jit(solution)/shard_map/ppermute | solution.py:299
  2.3 20.9 %all-to-all-start = ((s32[16,1,16]{2,1,0:T(1,128)}), s32[16,1,16]{2,1,0:T(1,128)S(1)}, u32[]{:S(2)}, u32[]{:S(2)}) async-start(s32[16,1,16]{2,1,0:T(1,128)} %bitcast.13), calls=%async_computation | async-start | bytes 16384 | tf_op jit(solution)/shard_map/all_to_all | solution.py:289
  24.3 16.8 %all-to-all-start.1 = ((bf16[16,16,512]{2,1,0:T(8,128)(2,1)}), bf16[16,16,512]{2,1,0:T(8,128)(2,1)S(1)}, u32[]{:S(2)}, u32[]{:S(2)}) async-start(bf16[16,16,512]{2,1,0:T(8,128)(2,1)} %bitcast.4), calls=%async_computation.1 | async-start | bytes 524288 | tf_op jit(solution)/shard_map/all_to_all | solution.py:328

commit v2 on v1

--- a/solution.py
+++ b/solution.py
@@ -9,6 +9,7 @@
 
 HALO = 256
 BLOCK = 512
+LANES = 128
 F32, BF16 = jnp.float32, jnp.bfloat16
 NN = (((1,), (0,)), ((), ()))
 NT = (((1,), (1,)), ((), ()))
@@ -20,8 +21,7 @@
     return lax.dot_general(a, b, dims, preferred_element_type=F32)
 
 
-def swish(v):
-    half = 0.5 * v
+def swish_of_half(half):
     return half * jnp.tanh(half) + half
 
 
@@ -48,7 +48,7 @@
     fa[...] = jnp.zeros(fa.shape, F32)
     wa[...] = jnp.zeros(wa.shape, F32)
     f_high, f_low = split(feats[...])
-    w_high, w_low = split(w_feat[...])
+    w_high, w_low = split(0.5 * w_feat[...])
     for at, (f, w) in enumerate(((f_high, w_high), (f_high, w_low), (f_low, w_high))):
         fa[at * rows : (at + 1) * rows, :] = f.astype(F32)
         wa[at * rows : (at + 1) * rows, :] = w.astype(F32)
@@ -71,7 +71,7 @@
     held = {}
 
     def first(i):
-        return to_of(i), swish(pre_of(i)).astype(BF16)
+        return to_of(i), swish_of_half(pre_of(i)).astype(BF16)
 
     def second(i, to, hidden):
         return to, mul(w_out, hidden, TN)
@@ -97,9 +97,8 @@
     return summed.astype(BF16)
 
 
-def nodes_of(latent, summed, w_in, w_out):
-    width = latent.shape[1]
-    hidden = swish(mul(latent, w_in[:width, :]) + mul(summed, w_in[width:, :])).astype(BF16)
+def nodes_of(latent, first, summed, w_in, w_out):
+    hidden = swish_of_half(0.5 * (first + mul(summed, w_in))).astype(BF16)
     centered, scale = norm(mul(hidden, w_out[...]), 1)
     return (latent.astype(F32) + centered * scale).astype(BF16)
 
@@ -118,71 +117,82 @@
     return jnp.sum(jnp.where(own, wide, 0.0), axis=0, keepdims=True).astype(jnp.int32)
 
 
-def band_ends(grid_any, pair_any, other_any, pair, other, sems, out_sems):
-    first = (lax.axis_index("tile") % 2) * (grid_any.shape[0] - HALO)
-    last = grid_any.shape[0] - HALO - first
-    fetch(
-        (
-            (grid_any.at[pl.ds(pl.multiple_of(last, HALO), HALO), :], pair),
-            (grid_any.at[pl.ds(pl.multiple_of(first, HALO), HALO), :], other),
-        ),
-        sems,
-    )(0, 1)
-    fetch(((pair, pair_any), (other, other_any)), out_sems)(0, 1)
+def band_ends(grid_any, grid, pair_any, other_any, sems, out_sems):
+    first = (lax.axis_index("tile") % 2) * (grid.shape[0] - HALO)
+    last = grid.shape[0] - HALO - first
+    size = grid.shape[0] // sems.shape[0]
+    spans = [pl.ds(i * size, size) for i in range(sems.shape[0])]
+    fetch([(grid_any.at[span, :], grid.at[span, :]) for span in spans], sems)(*range(len(spans)))
+    ends = [grid.at[pl.ds(pl.multiple_of(at, HALO), HALO), :] for at in (last, first)]
+    fetch(((ends[0], pair_any), (ends[1], other_any)), out_sems)(0, 1)
 
 
 def encode(
-    from_pair, from_other,
+    from_pair, from_other, grid,
     count_any, feats_any, sender_any, receiver_any, feat_any, latent_any, recv_any, send_any,
-    grid_any, out_any, in_any, node_any, next_any,
+    out_any, in_any, node_any, next_any,
     mid, sent,
-    count, feats, sender, receiver, w_feat, latent, w_recv, w_send, grid, w_out, w_in, w_node,
-    w_next, table, recv_table, fa, wa, sems,
+    count, sender, feats, receiver, w_feat, latent, w_recv, w_send, w_out, w_in, w_node,
+    w_next, first, table, picked, recv_table, fa, wa, sems,
 ):
     ready = fetch(
         (
-            (feats_any, feats), (feat_any, w_feat), (latent_any, latent), (recv_any, w_recv),
-            (send_any, w_send), (grid_any, grid), (sender_any, sender), (receiver_any, receiver),
-            (out_any, w_out), (count_any, count), (in_any, w_in), (node_any, w_node),
-            (next_any, w_next),
+            (sender_any, sender), (feats_any, feats), (feat_any, w_feat),
+            (latent_any, latent), (recv_any, w_recv), (send_any, w_send),
+            (receiver_any, receiver), (out_any, w_out), (count_any, count), (in_any, w_in),
+            (node_any, w_node), (next_any, w_next),
         ),
         sems,
     )
-    own = grid.shape[0]
-    ready(0, 1)
+    own, width = grid.shape
+    parts = width // LANES
+    odd = lax.axis_index("tile") % 2 == 1
+
+    def place_rows(at, rows):
+        for c in range(parts):
+            span = pl.ds(at * parts + c, rows.shape[0], stride=parts)
+            table[span, :] = rows[:, c * LANES : (c + 1) * LANES].astype(F32)
+
+    place_rows(0, jnp.where(odd, from_pair[...], from_other[...]))
+    place_rows(HALO + own, jnp.where(odd, from_other[...], from_pair[...]))
+    place_rows(HALO, grid[...])
+    ready(0)
+
+    def gather(i):
+        for e in range(i * BLOCK, (i + 1) * BLOCK):
+            row = table[pl.ds(sender[0, e] * parts, parts), :]
+            picked[pl.ds(e // 8 * (8 * parts) + e % 8, parts, stride=8), :] = row
+
+    gather(0)
+    ready(1, 2)
     stack_feats(feats, w_feat, fa, wa)
-    ready(2, 3)
-    recv_table[...] = mul(w_recv[...], latent[...], TT).astype(BF16)
-    ready(4)
-    table[:, :HALO] = mul(w_send[...], from_pair[...], TT).astype(BF16)
-    table[:, HALO : 2 * HALO] = mul(w_send[...], from_other[...], TT).astype(BF16)
-    ready(5)
-    table[:, 2 * HALO :] = mul(w_send[...], grid[...], TT).astype(BF16)
+    ready(3, 4)
+    recv_table[...] = (0.5 * mul(w_recv[...], latent[...], TT)).astype(BF16)
     wab = wa[...].astype(BF16)
-    ready(6, 7, 8, 9)
-    odd = lax.axis_index("tile") % 2
-    above, below = (1 - odd) * HALO, odd * HALO
+    ready(5, 6, 7, 8)
+    half_send = w_send[...] * jnp.array(0.5, BF16)
 
     def to_of(i):
         return places(recv_table.shape[1], receiver[:, pl.ds(i * BLOCK, BLOCK)])
 
     def pre_of(i):
         span = pl.ds(i * BLOCK, BLOCK)
-        s = sender[:, span]
-        s = jnp.where(
-            s < HALO,
-            s + above,
-            jnp.where(s < HALO + own, s + HALO, s - (HALO + own) + below),
-        )
-        pre = mul(table[...], places(table.shape[1], s))
+        size = BLOCK * parts
+        rows = picked[i * size : (i + 1) * size, :].reshape(BLOCK // 8, parts, 8, LANES)
+        rows = [rows[:, c].reshape(BLOCK, LANES).astype(BF16) for c in range(parts)]
+        pre = mul(half_send, jnp.concatenate(rows, axis=1), TT)
+        if (i + 1) * BLOCK < picked.shape[0] // parts:
+            gather(i + 1)
         pre += mul(recv_table[...], to_of(i))
         return pre + mul(wab, fa[:, span].astype(BF16), TN)
 
-    summed = summed_messages(sender.shape[1], pre_of, to_of, w_out, count[0])
-    ready(10, 11, 12)
-    middle = nodes_of(latent[...], summed, w_in, w_node)
+    ready(9)
+    first[...] = mul(latent[...], w_in[:width, :])
+    summed = summed_messages(receiver.shape[1], pre_of, to_of, w_out, count[0])
+    ready(10, 11)
+    middle = nodes_of(latent[...], first[...], summed, w_in[width:, :], w_node)
     mid[...] = middle
-    sent[...] = mul(middle, w_next[...]).astype(BF16)
+    sent[...] = (0.5 * mul(middle, w_next[...])).astype(BF16)
 
 
 def answer(sent, asked, outgoing_any, outgoing, rows, sems):
@@ -192,41 +202,46 @@
 
 
 def process_own(
-    mid, feats_any, receiver_any, feat_any, recv_any, pre,
-    feats, receiver, w_feat, w_recv, recv_table, fa, wa, sems,
+    mid, feats_any, receiver_any, feat_any, recv_any, in_any, out_any, pre, w_out, first_any,
+    feats, receiver, w_feat, w_recv, w_in, first, recv_table, fa, wa, sems, out_sems,
 ):
     ready = fetch(
         (
             (feats_any, feats), (feat_any, w_feat), (recv_any, w_recv), (receiver_any, receiver),
+            (in_any.at[: w_in.shape[0], :], w_in), (out_any, w_out),
         ),
         sems,
     )
     ready(0, 1)
     stack_feats(feats, w_feat, fa, wa)
     ready(2)
-    recv_table[...] = mul(w_recv[...], mid[...], TT).astype(BF16)
+    recv_table[...] = (0.5 * mul(w_recv[...], mid[...], TT)).astype(BF16)
     wab = wa[...].astype(BF16)
     ready(3)
     for start in range(0, pre.shape[1], BLOCK):
         span = pl.ds(start, BLOCK)
         part = mul(recv_table[...], places(recv_table.shape[1], receiver[:, span]))
         pre[:, span] = (part + mul(wab, fa[:, span].astype(BF16), TN)).astype(pre.dtype)
+    ready(4)
+    first[...] = mul(mid[...], w_in[...])
+    fetch(((first, first_any),), out_sems)(0)
+    ready(5)
 
 
 def process_rest(
-    mid, pre, listed, count_any, sender_any, receiver_any, out_any, in_any, node_any,
+    mid, pre, listed, w_out, count_any, sender_any, receiver_any, first_any, in_any, node_any,
     result_any,
-    count, sender, receiver, w_out, w_in, w_node, result, sems, out_sems,
+    count, sender, receiver, first, w_in, w_node, result, sems, out_sems,
 ):
     ready = fetch(
         (
-            (sender_any, sender), (receiver_any, receiver), (count_any, count), (out_any, w_out),
-            (in_any, w_in), (node_any, w_node),
+            (sender_any, sender), (receiver_any, receiver), (count_any, count),
+            (first_any, first), (in_any.at[w_in.shape[0] :, :], w_in), (node_any, w_node),
         ),
         sems,
     )
     table = listed[...].T
-    ready(0, 1, 2, 3)
+    ready(0, 1, 2)
 
     def to_of(i):
         return places(mid.shape[0], receiver[:, pl.ds(i * BLOCK, BLOCK)])
@@ -236,13 +251,16 @@
         return pre[:, span] + mul(table, places(table.shape[1], sender[:, span]))
 
     summed = summed_messages(sender.shape[1], pre_of, to_of, w_out, count[0])
-    ready(4, 5)
-    result[...] = nodes_of(mid[...], summed, w_in, w_node)
+    ready(3, 4, 5)
+    result[...] = nodes_of(mid[...], first[...], summed, w_in[...], w_node)
     fetch(((result, result_any),), out_sems)(0)
 
 
 S, V, H = (pl.BlockSpec(memory_space=m) for m in (pltpu.SMEM, pltpu.VMEM, pltpu.HBM))
-ONE = "one integer"
+
+
+class Scalars(jax.ShapeDtypeStruct):
+    pass
 
 
 def shape(*sizes, dtype=BF16):
@@ -256,7 +274,7 @@
         in_specs=[V] * len(near) + [H] * len(far),
         out_specs=[V] * len(near_outs) + [H] * len(far_outs),
         scratch_shapes=[
-            pltpu.SMEM((1,), jnp.int32) if s is ONE else pltpu.VMEM(s.shape, s.dtype)
+            (pltpu.SMEM if isinstance(s, Scalars) else pltpu.VMEM)(s.shape, s.dtype)
             for s in scratch
         ]
         + [pltpu.SemaphoreType.DMA((n,)) for n in copies],
@@ -277,6 +295,7 @@
     blocks = lax.axis_size("tile")
     per = need_rows.shape[2]
     square = shape(width, width)
+    one, scalars = (Scalars(n, jnp.int32) for n in ((1,), (1, slots)))
     node_rows = shape(nodes, width)
     edge_index = shape(1, slots, dtype=jnp.int32)
     edge_feats = shape(*enc_feats.shape, dtype=F32)
@@ -289,9 +308,15 @@
     asked = lax.all_to_all(
         need_rows.reshape(blocks, 1, per), "tile", split_axis=0, concat_axis=0, tiled=True
     )
-    for_pair, for_other = call(
-        band_ends, "band_ends", [], [grid_latent], [], [shape(HALO, width)] * 2,
-        [shape(HALO, width)] * 2, (2, 2),
+    grid, for_pair, for_other = call(
+        band_ends,
+        "band_ends",
+        [],
+        [grid_latent],
+        [shape(rows, width)],
+        [shape(HALO, width)] * 2,
+        [],
+        (4, 2),
     )
     pairs = [(i, i ^ 1) for i in range(blocks)]
     others = [(i, i + 1 if i % 2 else i - 1) for i in range(1, blocks - 1)]
@@ -300,20 +325,21 @@
     mid, sent = call(
         encode,
         "encode",
-        [from_pair, from_other],
+        [from_pair, from_other, grid],
         [
             enc_count, enc_feats, enc_sender, enc_receiver, w_enc_feat, mesh_latent, w_enc_recv,
-            w_enc_send, grid_latent, w_enc_out, w_enc_node_in, w_enc_node_out, w_proc_send,
+            w_enc_send, w_enc_out, w_enc_node_in, w_enc_node_out, w_proc_send,
         ],
         [node_rows, node_rows],
         [],
         [
-            ONE, edge_feats, edge_index, edge_index, feat_weight, node_rows, square, square,
-            shape(rows, width), square, shape(2 * width, width), square, square,
-            shape(width, rows + 2 * HALO), shape(width, nodes),
+            one, scalars, edge_feats, edge_index, feat_weight, node_rows, square, square,
+            square, shape(2 * width, width), square, square, shape(nodes, width, dtype=F32),
+            shape((rows + 2 * HALO) * width // LANES, LANES, dtype=F32),
+            shape(slots * width // LANES, LANES, dtype=F32), shape(width, nodes),
         ]
         + stacked,
-        (13,),
+        (12,),
     )
     (outgoing,) = call(
         answer,
@@ -328,27 +354,30 @@
     listed = lax.all_to_all(
         outgoing.reshape(blocks, per, width), "tile", split_axis=0, concat_axis=0, tiled=True
     ).reshape(blocks * per, width)
-    (pre,) = call(
+    pre, w_out, first = call(
         process_own,
         "process_own",
         [mid],
-        [mesh_feats, mesh_receiver, w_proc_feat, w_proc_recv],
-        [shape(width, slots)],
-        [],
-        [edge_feats, edge_index, feat_weight, square, shape(width, nodes)] + stacked,
-        (4,),
+        [mesh_feats, mesh_receiver, w_proc_feat, w_proc_recv, w_proc_node_in, w_proc_out],
+        [shape(width, slots), square],
+        [shape(nodes, width, dtype=F32)],
+        [
+            edge_feats, edge_index, feat_weight, square, square,
+            shape(nodes, width, dtype=F32), shape(width, nodes),
+        ]
+        + stacked,
+        (6, 1),
     )
     (result,) = call(
         process_rest,
         "process_rest",
-        [mid, pre, listed],
-        [
-            mesh_count, mesh_sender, mesh_receiver, w_proc_out, w_proc_node_in, w_proc_node_out,
-        ],
+        [mid, pre, listed, w_out],
+        [mesh_count, mesh_sender, mesh_receiver, first, w_proc_node_in, w_proc_node_out],
         [],
         [node_rows],
         [
-            ONE, edge_index, edge_index, square, shape(2 * width, width), square, node_rows,
+            one, edge_index, edge_index, shape(nodes, width, dtype=F32), square, square,
+            node_rows,
         ],
         (6, 1),
     )

time: 47.5 us -> 43.8 us (0.922)
  Pallas kernels: 22.2 us -> 19 us
  waiting for transfers between devices: 6.71 us -> 5.28 us
  local copies, waits for them, and re-layouts: 0 us -> 0.79 us
    pallas_call x5, Pallas kernels: 22.2 us -> 19 us  [call(): pl.pallas_call(kernel, out_shape=near_outs + far_outs, in_specs=[V] * len...]
    all_to_all x1, waiting for transfers between devices: 6.7 us -> 5.27 us  [body(): lax.all_to_all(outgoing.reshape(blocks, per, width), 'tile', split_axis=0...]
    unnamed x0 -> x2, local copies, waits for them, and re-layouts: none -> 0.79 us
  transfers between devices with their start and end apart: 4 -> 4, of which waited for: 1 -> 1; matrix products, arithmetic and copies ran while one was open for 0% -> 0% of each run, Pallas kernels for 30% -> 27%
where the time goes in v2:
time: 43.8 us; the launch traced here: 43.3 us
  Pallas kernels  19 us (43%)
  starting transfers between devices  16.7 us (38%)
  waiting for transfers between devices  5.28 us (12%)
  between operations  1.54 us (4%)
  local copies, waits for them, and re-layouts  0.79 us (2%)
    pallas_call x5, Pallas kernels, call(): pl.pallas_call(kernel, out_shape=near_outs + far_outs, in_specs=[V] * len...  19 us
    all_to_all x1, starting transfers between devices, body(): lax.all_to_all(need_rows.reshape(blocks, 1, per), 'tile', split_axis=0, c...  8.8 us
    all_to_all x1, starting transfers between devices, body(): lax.all_to_all(outgoing.reshape(blocks, per, width), 'tile', split_axis=0...  6.75 us
    all_to_all x1, waiting for transfers between devices, body(): lax.all_to_all(outgoing.reshape(blocks, per, width), 'tile', split_axis=0...  5.27 us
  transfers between devices with their start and end apart: 4, of which 1 were waited for; matrix products, arithmetic and copies ran while one was open for 0% of the time, Pallas kernels for 27%

profile of v2, /device:TPU:0, one launch (start us, length us, event | category | flops | bytes accessed | tf_op | source)
XLA Modules:
  0.0 43.3 jit_solution(410360928768976104)
XLA Ops:
  0.0 1.3 %band_ends.1 = (bf16[1024,512]{1,0:T(8,128)(2,1)S(1)}, bf16[256,512]{1,0:T(8,128)(2,1)S(1)}, bf16[256,512]{1,0:T(8,128)(2,1)S(1)}) custom-call(bf16[1024,512]{1,0:T(8,128)(2,1)} %grid_any.1), custom_call_target="tpu_custom_call" | custom-call | tf_op jit(solution)/shard_map/band_ends/pallas_call | solution.py:271
  1.3 0.5 %collective-permute-start = (bf16[256,512]{1,0:T(8,128)(2,1)S(1)}, bf16[256,512]{1,0:T(8,128)(2,1)S(1)}, u32[]{:S(2)}, u32[]{:S(2)}) collective-permute-start(bf16[256,512]{1,0:T(8,128)(2,1)S(1)} %get-tuple-element.13), channel_id=1, source_target_pairs={{0,1},{1,0},{2,3},{3,2},{4,5},{5,4},{6,7},{7,6},{8,9},{9,8},{10,11... | collective-permute-start | bytes 786440 | tf_op jit(solution)/shard_map/ppermute | solution.py:323
  1.8 0.7 %collective-permute-start.1 = (bf16[256,512]{1,0:T(8,128)(2,1)S(1)}, bf16[256,512]{1,0:T(8,128)(2,1)S(1)}, u32[]{:S(2)}, u32[]{:S(2)}) collective-permute-start(bf16[256,512]{1,0:T(8,128)(2,1)S(1)} %get-tuple-element.14), channel_id=1, source_target_pairs={{1,2},{2,1},{3,4},{4,3},{5,6},{6,5},{7,8},{8,7},{9,10},{10,9},{11,... | collective-permute-start | bytes 786440 | tf_op jit(solution)/shard_map/ppermute | solution.py:324
  2.5 8.8 %all-to-all-start = ((s32[16,1,16]{2,1,0:T(1,128)}), s32[16,1,16]{2,1,0:T(1,128)S(1)}, u32[]{:S(2)}, u32[]{:S(2)}) async-start(s32[16,1,16]{2,1,0:T(1,128)} %bitcast.13), calls=%async_computation | async-start | bytes 16384 | tf_op jit(solution)/shard_map/all_to_all | solution.py:308
  11.9 0.0 collective-permute-done.from_pair
  11.9 0.0 collective-permute-done.1.from_other
  11.9 8.2 %encode.1 = (bf16[256,512]{1,0:T(8,128)(2,1)S(1)}, bf16[256,512]{1,0:T(8,128)(2,1)S(1)}) custom-call(bf16[256,512]{1,0:T(8,128)(2,1)S(1)} %collective-permute-done.from_pair, bf16[256,512]{1,0:T(8,128)(2,1)S(1)} %collective-permute-done.1.from_other, bf16[1024,512]{1,0:T(8,128)(2,1)S(1)} %get-tuple-element.15.grid, s32[1]{0:T(128)S(6)} %copy.24.count_any, ...), custom_call_target="tpu_custom_call" | custom-call | tf_op jit(solution)/shard_map/encode/pallas_call | solution.py:271
  20.1 0.0 all-to-all-done.asked
  20.1 1.1 %answer.1 = bf16[256,512]{1,0:T(8,128)(2,1)} custom-call(bf16[256,512]{1,0:T(8,128)(2,1)S(1)} %get-tuple-element.18.sent, s32[16,1,16]{2,1,0:T(1,128)S(1)} %all-to-all-done.asked), custom_call_target="tpu_custom_call" | custom-call | tf_op jit(solution)/shard_map/answer/pallas_call | solution.py:271
  21.3 6.8 %all-to-all-start.1 = ((bf16[16,16,512]{2,1,0:T(8,128)(2,1)}), bf16[16,16,512]{2,1,0:T(8,128)(2,1)S(1)}, u32[]{:S(2)}, u32[]{:S(2)}) async-start(bf16[16,16,512]{2,1,0:T(8,128)(2,1)} %bitcast.4), calls=%async_computation.1 | async-start | bytes 524288 | tf_op jit(solution)/shard_map/all_to_all | solution.py:354
  28.7 3.3 %process_own.1 = (bf16[512,2048]{1,0:T(8,128)(2,1)S(1)}, bf16[512,512]{1,0:T(8,128)(2,1)S(1)}, f32[256,512]{1,0:T(8,128)S(1)}) custom-call(bf16[256,512]{1,0:T(8,128)(2,1)S(1)} %get-tuple-element.16.mid, f32[4,2048]{1,0:T(4,128)} %feats_any.3, s32[1,2048]{1,0:T(1,128)} %bitcast.8, f32[4,512]{1,0:T(4,128)} %feat_any.3, bf16[512,512]{1,0:T(8,128)(2,1)} %recv_any.3, ...), custom_call_target="tpu_custom_call" | custom-call | tf_op jit(solution)/shard_map/process_own/pallas_call | solution.py:271
  32.0 0.0 copy-start
  32.0 0.8 %copy-done = f32[256,512]{1,0:T(8,128)} copy-done((f32[256,512]{1,0:T(8,128)}, f32[256,512]{1,0:T(8,128)S(1)}, u32[]{:S(2)}) %copy-start) | copy-done | bytes 524312
  32.8 5.3 %all-to-all-done.1 = bf16[16,16,512]{2,1,0:T(8,128)(2,1)S(1)} async-done(((bf16[16,16,512]{2,1,0:T(8,128)(2,1)}), bf16[16,16,512]{2,1,0:T(8,128)(2,1)S(1)}, u32[]{:S(2)}, u32[]{:S(2)}) %all-to-all-start.1) | async-done | bytes 262176 | tf_op jit(solution)/shard_map/all_to_all | solution.py:354
  38.1 5.1 %process_rest.1 = bf16[256,512]{1,0:T(8,128)(2,1)} custom-call(bf16[256,512]{1,0:T(8,128)(2,1)S(1)} %get-tuple-element.16.mid, bf16[512,2048]{1,0:T(8,128)(2,1)S(1)} %get-tuple-element.17.pre, bf16[256,512]{1,0:T(8,128)(2,1)S(1)} %bitcast.7, bf16[512,512]{1,0:T(8,128)(2,1)S(1)} %get-tuple-element.19.w_out, s32[1]{0:T(128)S(6)} %copy.25.count_any, ...), custom_call_target="tpu_custom_call" | custom-call | tf_op jit(solution)/shard_map/process_rest/pallas_call | solution.py:271
Async XLA Ops:
  1.3 10.6 %collective-permute-start = (bf16[256,512]{1,0:T(8,128)(2,1)S(1)}, bf16[256,512]{1,0:T(8,128)(2,1)S(1)}, u32[]{:S(2)}, u32[]{:S(2)}) collective-permute-start(bf16[256,512]{1,0:T(8,128)(2,1)S(1)} %get-tuple-element.13), channel_id=1, source_target_pairs={{0,1},{1,0},{2,3},{3,2},{4,5},{5,4},{6,7},{7,6},{8,9},{9,8},{10,11... | collective-permute-start | bytes 786440 | tf_op jit(solution)/shard_map/ppermute | solution.py:323
  1.8 10.1 %collective-permute-start.1 = (bf16[256,512]{1,0:T(8,128)(2,1)S(1)}, bf16[256,512]{1,0:T(8,128)(2,1)S(1)}, u32[]{:S(2)}, u32[]{:S(2)}) collective-permute-start(bf16[256,512]{1,0:T(8,128)(2,1)S(1)} %get-tuple-element.14), channel_id=1, source_target_pairs={{1,2},{2,1},{3,4},{4,3},{5,6},{6,5},{7,8},{8,7},{9,10},{10,9},{11,... | collective-permute-start | bytes 786440 | tf_op jit(solution)/shard_map/ppermute | solution.py:324
  2.5 17.7 %all-to-all-start = ((s32[16,1,16]{2,1,0:T(1,128)}), s32[16,1,16]{2,1,0:T(1,128)S(1)}, u32[]{:S(2)}, u32[]{:S(2)}) async-start(s32[16,1,16]{2,1,0:T(1,128)} %bitcast.13), calls=%async_computation | async-start | bytes 16384 | tf_op jit(solution)/shard_map/all_to_all | solution.py:308
  21.3 16.8 %all-to-all-start.1 = ((bf16[16,16,512]{2,1,0:T(8,128)(2,1)}), bf16[16,16,512]{2,1,0:T(8,128)(2,1)S(1)}, u32[]{:S(2)}, u32[]{:S(2)}) async-start(bf16[16,16,512]{2,1,0:T(8,128)(2,1)} %bitcast.4), calls=%async_computation.1 | async-start | bytes 524288 | tf_op jit(solution)/shard_map/all_to_all | solution.py:354
  32.0 0.8 %copy-start = (f32[256,512]{1,0:T(8,128)}, f32[256,512]{1,0:T(8,128)S(1)}, u32[]{:S(2)}) copy-start(f32[256,512]{1,0:T(8,128)S(1)} %get-tuple-element.20.first_any) | copy-start | bytes 1572868

commit v3 on v2

--- a/solution.py
+++ b/solution.py
@@ -10,6 +10,7 @@
 HALO = 256
 BLOCK = 512
 LANES = 128
+SPARE = 64
 F32, BF16 = jnp.float32, jnp.bfloat16
 NN = (((1,), (0,)), ((), ()))
 NT = (((1,), (1,)), ((), ()))
@@ -77,9 +78,13 @@
         return to, mul(w_out, hidden, TN)
 
     def third(i, to, out):
-        out, scale = norm(out, 0)
+        one, part = out[:1, :], 1.0 / out.shape[0]
+        moved = out - one
+        mean = jnp.sum(moved, axis=0, keepdims=True) * part
+        variance = jnp.sum(moved * moved, axis=0, keepdims=True) * part - mean * mean
+        scale = lax.rsqrt(jnp.maximum(variance, 0.0) + 1e-05)
         live = lax.broadcasted_iota(jnp.int32, (1, BLOCK), 1) + i * BLOCK < count
-        return to, (out * jnp.where(live, scale, 0.0)).astype(BF16)
+        return to, ((out - (mean + one)) * jnp.where(live, scale, 0.0)).astype(BF16)
 
     def last(i, to, message):
         return (mul(to, message, NT),)
@@ -103,48 +108,47 @@
     return (latent.astype(F32) + centered * scale).astype(BF16)
 
 
-def in_a_row(asked, rows):
+def in_a_column(asked):
     blocks, _, per = asked.shape
-    for i in range(blocks):
-        rows[i : i + 1, :] = asked[i].astype(F32)
-    size = (per, blocks * per)
-    column = lax.broadcasted_iota(jnp.int32, size, 1) % per
-    repeat = (column == lax.broadcasted_iota(jnp.int32, size, 0)).astype(F32).astype(BF16)
-    wide = mul(rows[...].astype(BF16), repeat)
-    size = wide.shape
-    block = lax.broadcasted_iota(jnp.int32, size, 1) // per
-    own = block == lax.broadcasted_iota(jnp.int32, size, 0)
-    return jnp.sum(jnp.where(own, wide, 0.0), axis=0, keepdims=True).astype(jnp.int32)
-
-
-def band_ends(grid_any, grid, pair_any, other_any, sems, out_sems):
-    first = (lax.axis_index("tile") % 2) * (grid.shape[0] - HALO)
-    last = grid.shape[0] - HALO - first
-    size = grid.shape[0] // sems.shape[0]
-    spans = [pl.ds(i * size, size) for i in range(sems.shape[0])]
-    fetch([(grid_any.at[span, :], grid.at[span, :]) for span in spans], sems)(*range(len(spans)))
-    ends = [grid.at[pl.ds(pl.multiple_of(at, HALO), HALO), :] for at in (last, first)]
-    fetch(((ends[0], pair_any), (ends[1], other_any)), out_sems)(0, 1)
+    size = (blocks, per, per)
+    own = lax.broadcasted_iota(jnp.int32, size, 1) == lax.broadcasted_iota(jnp.int32, size, 2)
+    column = jnp.sum(jnp.where(own, asked.astype(F32), 0.0), axis=2, keepdims=True)
+    return column.reshape(blocks * per, 1).astype(jnp.int32)
+
+
+def band_ends(
+    grid_any, latent_any, feats_any, receiver_any,
+    pair, other, middle, latent, feats, receiver, sems,
+):
+    last = grid_any.shape[0] - HALO
+    first = (lax.axis_index("tile") % 2) * last
+    pair_at, other_at = (pl.ds(pl.multiple_of(at, HALO), HALO) for at in (last - first, first))
+    fetch(
+        (
+            (grid_any.at[pair_at, :], pair), (grid_any.at[other_at, :], other),
+            (grid_any.at[HALO:last, :], middle), (latent_any, latent), (feats_any, feats),
+            (receiver_any, receiver),
+        ),
+        sems,
+    )(*range(6))
 
 
 def encode(
-    from_pair, from_other, grid,
-    count_any, feats_any, sender_any, receiver_any, feat_any, latent_any, recv_any, send_any,
-    out_any, in_any, node_any, next_any,
+    from_pair, from_other, pair, other, middle, latent, feats, receiver,
+    count_any, sender_any, feat_any, recv_any, send_any, out_any, in_any, node_any, next_any,
     mid, sent,
-    count, sender, feats, receiver, w_feat, latent, w_recv, w_send, w_out, w_in, w_node,
-    w_next, first, table, picked, recv_table, fa, wa, sems,
+    count, sender, w_feat, w_recv, w_send, w_out, w_in, w_node, w_next,
+    first, table, picked, recv_table, fa, wa, sems,
 ):
     ready = fetch(
         (
-            (sender_any, sender), (feats_any, feats), (feat_any, w_feat),
-            (latent_any, latent), (recv_any, w_recv), (send_any, w_send),
-            (receiver_any, receiver), (out_any, w_out), (count_any, count), (in_any, w_in),
-            (node_any, w_node), (next_any, w_next),
+            (sender_any, sender), (feat_any, w_feat), (recv_any, w_recv), (send_any, w_send),
+            (out_any, w_out), (count_any, count), (in_any, w_in), (node_any, w_node),
+            (next_any, w_next),
         ),
         sems,
     )
-    own, width = grid.shape
+    own, width = middle.shape[0] + 2 * HALO, middle.shape[1]
     parts = width // LANES
     odd = lax.axis_index("tile") % 2 == 1
 
@@ -153,10 +157,12 @@
             span = pl.ds(at * parts + c, rows.shape[0], stride=parts)
             table[span, :] = rows[:, c * LANES : (c + 1) * LANES].astype(F32)
 
+    place_rows(2 * HALO, middle[...])
+    place_rows(HALO, jnp.where(odd, pair[...], other[...]))
+    place_rows(own, jnp.where(odd, other[...], pair[...]))
     place_rows(0, jnp.where(odd, from_pair[...], from_other[...]))
     place_rows(HALO + own, jnp.where(odd, from_other[...], from_pair[...]))
-    place_rows(HALO, grid[...])
-    ready(0)
+    ready(0, 1)
 
     def gather(i):
         for e in range(i * BLOCK, (i + 1) * BLOCK):
@@ -164,12 +170,11 @@
             picked[pl.ds(e // 8 * (8 * parts) + e % 8, parts, stride=8), :] = row
 
     gather(0)
-    ready(1, 2)
     stack_feats(feats, w_feat, fa, wa)
-    ready(3, 4)
+    ready(2)
     recv_table[...] = (0.5 * mul(w_recv[...], latent[...], TT)).astype(BF16)
     wab = wa[...].astype(BF16)
-    ready(5, 6, 7, 8)
+    ready(3, 4, 5)
     half_send = w_send[...] * jnp.array(0.5, BF16)
 
     def to_of(i):
@@ -181,24 +186,35 @@
         rows = picked[i * size : (i + 1) * size, :].reshape(BLOCK // 8, parts, 8, LANES)
         rows = [rows[:, c].reshape(BLOCK, LANES).astype(BF16) for c in range(parts)]
         pre = mul(half_send, jnp.concatenate(rows, axis=1), TT)
-        if (i + 1) * BLOCK < picked.shape[0] // parts:
+        if (i + 1) * BLOCK < receiver.shape[1]:
             gather(i + 1)
         pre += mul(recv_table[...], to_of(i))
         return pre + mul(wab, fa[:, span].astype(BF16), TN)
 
-    ready(9)
+    ready(6)
     first[...] = mul(latent[...], w_in[:width, :])
     summed = summed_messages(receiver.shape[1], pre_of, to_of, w_out, count[0])
-    ready(10, 11)
+    ready(7, 8)
     middle = nodes_of(latent[...], first[...], summed, w_in[width:, :], w_node)
     mid[...] = middle
     sent[...] = (0.5 * mul(middle, w_next[...])).astype(BF16)
 
 
-def answer(sent, asked, outgoing_any, outgoing, rows, sems):
-    at = places(sent.shape[0], in_a_row(asked, rows))
-    outgoing[...] = mul(at, sent[...], TN).astype(BF16)
-    fetch(((outgoing, outgoing_any),), sems)(0)
+def answer(sent, asked, outgoing_any, outgoing, sems):
+    column = in_a_column(asked[...])
+    size = (column.shape[0], sent.shape[0])
+    at = (lax.broadcasted_iota(jnp.int32, size, 1) == column).astype(F32).astype(BF16)
+    part = size[0] // sems.shape[0]
+    copies = []
+    for i in range(sems.shape[0]):
+        span = pl.ds(i * part, part)
+        outgoing[span, :] = mul(at[i * part : (i + 1) * part, :], sent[...]).astype(BF16)
+        copies.append(
+            pltpu.make_async_copy(outgoing.at[span, :], outgoing_any.at[span, :], sems.at[i])
+        )
+        copies[-1].start()
+    for copy in copies:
+        copy.wait()
 
 
 def process_own(
@@ -308,16 +324,20 @@
     asked = lax.all_to_all(
         need_rows.reshape(blocks, 1, per), "tile", split_axis=0, concat_axis=0, tiled=True
     )
-    grid, for_pair, for_other = call(
+    near = call(
         band_ends,
         "band_ends",
         [],
-        [grid_latent],
-        [shape(rows, width)],
-        [shape(HALO, width)] * 2,
-        [],
-        (4, 2),
-    )
+        [grid_latent, mesh_latent, enc_feats, enc_receiver],
+        [
+            shape(HALO, width), shape(HALO, width), shape(rows - 2 * HALO, width), node_rows,
+            edge_feats, edge_index,
+        ],
+        [],
+        [],
+        (6,),
+    )
+    for_pair, for_other = near[:2]
     pairs = [(i, i ^ 1) for i in range(blocks)]
     others = [(i, i + 1 if i % 2 else i - 1) for i in range(1, blocks - 1)]
     from_pair = lax.ppermute(for_pair, "tile", pairs)
@@ -325,21 +345,22 @@
     mid, sent = call(
         encode,
         "encode",
-        [from_pair, from_other, grid],
+        [from_pair, from_other, *near],
         [
-            enc_count, enc_feats, enc_sender, enc_receiver, w_enc_feat, mesh_latent, w_enc_recv,
-            w_enc_send, w_enc_out, w_enc_node_in, w_enc_node_out, w_proc_send,
+            enc_count, enc_sender, w_enc_feat, w_enc_recv, w_enc_send, w_enc_out, w_enc_node_in,
+            w_enc_node_out, w_proc_send,
         ],
         [node_rows, node_rows],
         [],
         [
-            one, scalars, edge_feats, edge_index, feat_weight, node_rows, square, square,
-            square, shape(2 * width, width), square, square, shape(nodes, width, dtype=F32),
-            shape((rows + 2 * HALO) * width // LANES, LANES, dtype=F32),
-            shape(slots * width // LANES, LANES, dtype=F32), shape(width, nodes),
+            one, scalars, feat_weight, square, square, square, shape(2 * width, width), square,
+            square,
+            shape(nodes, width, dtype=F32),
+            shape((rows + 2 * HALO) * width // LANES + SPARE, LANES, dtype=F32),
+            shape(slots * width // LANES + SPARE, LANES, dtype=F32), shape(width, nodes),
         ]
         + stacked,
-        (12,),
+        (9,),
     )
     (outgoing,) = call(
         answer,
@@ -348,8 +369,8 @@
         [],
         [],
         [shape(blocks * per, width)],
-        [shape(blocks * per, width), shape(blocks, per, dtype=F32)],
-        (1,),
+        [shape(blocks * per, width)],
+        (2,),
     )
     listed = lax.all_to_all(
         outgoing.reshape(blocks, per, width), "tile", split_axis=0, concat_axis=0, tiled=True

time: 43.8 us -> 43.6 us (level)
  no operation moved by 1% of the time
where the time goes in v3:
time: 43.6 us; the launch traced here: 43.2 us
  Pallas kernels  18.8 us (43%)
  starting transfers between devices  16.7 us (38%)
  waiting for transfers between devices  5.28 us (12%)
  between operations  1.54 us (4%)
  local copies, waits for them, and re-layouts  0.79 us (2%)
    pallas_call x5, Pallas kernels, call(): pl.pallas_call(kernel, out_shape=near_outs + far_outs, in_specs=[V] * len...  18.8 us
    all_to_all x1, starting transfers between devices, body(): lax.all_to_all(need_rows.reshape(blocks, 1, per), 'tile', split_axis=0, c...  8.8 us
    all_to_all x1, starting transfers between devices, body(): lax.all_to_all(outgoing.reshape(blocks, per, width), 'tile', split_axis=0...  6.73 us
    all_to_all x1, waiting for transfers between devices, body(): lax.all_to_all(outgoing.reshape(blocks, per, width), 'tile', split_axis=0...  5.28 us
  transfers between devices with their start and end apart: 4, of which 1 were waited for; matrix products, arithmetic and copies ran while one was open for 0% of the time, Pallas kernels for 27%

profile of v3, /device:TPU:0, one launch (start us, length us, event | category | flops | bytes accessed | tf_op | source)
XLA Modules:
  0.0 43.2 jit_solution(15082645051639828516)
XLA Ops:
  0.0 1.3 %band_ends.1 = (bf16[256,512]{1,0:T(8,128)(2,1)S(1)}, bf16[256,512]{1,0:T(8,128)(2,1)S(1)}, bf16[512,512]{1,0:T(8,128)(2,1)S(1)}, bf16[256,512]{1,0:T(8,128)(2,1...) custom-call(bf16[1024,512]{1,0:T(8,128)(2,1)} %grid_any.1, bf16[256,512]{1,0:T(8,128)(2,1)} %latent_any.1, ...), custom_call_target="tpu_custom_call" | custom-call | tf_op jit(solution)/shard_map/band_ends/pallas_call | solution.py:287
  1.3 0.5 %collective-permute-start = (bf16[256,512]{1,0:T(8,128)(2,1)S(1)}, bf16[256,512]{1,0:T(8,128)(2,1)S(1)}, u32[]{:S(2)}, u32[]{:S(2)}) collective-permute-start(bf16[256,512]{1,0:T(8,128)(2,1)S(1)} %get-tuple-element.16.pair), channel_id=1, source_target_pairs={{0,1},{1,0},{2,3},{3,2},{4,5},{5,4},{6,7},{7,6},{8,9},{9,8},{10,11... | collective-permute-start | bytes 786440 | tf_op jit(solution)/shard_map/ppermute | solution.py:343
  1.8 0.7 %collective-permute-start.1 = (bf16[256,512]{1,0:T(8,128)(2,1)S(1)}, bf16[256,512]{1,0:T(8,128)(2,1)S(1)}, u32[]{:S(2)}, u32[]{:S(2)}) collective-permute-start(bf16[256,512]{1,0:T(8,128)(2,1)S(1)} %get-tuple-element.17.other), channel_id=1, source_target_pairs={{1,2},{2,1},{3,4},{4,3},{5,6},{6,5},{7,8},{8,7},{9,10},{10,9},{11,... | collective-permute-start | bytes 786440 | tf_op jit(solution)/shard_map/ppermute | solution.py:344
  2.5 8.8 %all-to-all-start = ((s32[16,1,16]{2,1,0:T(1,128)}), s32[16,1,16]{2,1,0:T(1,128)S(1)}, u32[]{:S(2)}, u32[]{:S(2)}) async-start(s32[16,1,16]{2,1,0:T(1,128)} %bitcast.13), calls=%async_computation | async-start | bytes 16384 | tf_op jit(solution)/shard_map/all_to_all | solution.py:324
  12.0 0.0 collective-permute-done.from_pair
  12.0 0.0 collective-permute-done.1.from_other
  12.0 8.2 %encode.1 = (bf16[256,512]{1,0:T(8,128)(2,1)S(1)}, bf16[256,512]{1,0:T(8,128)(2,1)S(1)}) custom-call(bf16[256,512]{1,0:T(8,128)(2,1)S(1)} %collective-permute-done.from_pair, bf16[256,512]{1,0:T(8,128)(2,1)S(1)} %collective-permute-done.1.from_other, bf16[256,512]{1,0:T(8,128)(2,1)S(1)} %get-tuple-element.16.pair, ...), custom_call_target="tpu_custom_call" | custom-call | tf_op jit(solution)/shard_map/encode/pallas_call | solution.py:287
  20.2 0.0 all-to-all-done.asked
  20.2 1.0 %answer.1 = bf16[256,512]{1,0:T(8,128)(2,1)} custom-call(bf16[256,512]{1,0:T(8,128)(2,1)S(1)} %get-tuple-element.24.sent, s32[16,1,16]{2,1,0:T(1,128)S(1)} %all-to-all-done.asked), custom_call_target="tpu_custom_call" | custom-call | tf_op jit(solution)/shard_map/answer/pallas_call | solution.py:287
  21.2 6.7 %all-to-all-start.1 = ((bf16[16,16,512]{2,1,0:T(8,128)(2,1)}), bf16[16,16,512]{2,1,0:T(8,128)(2,1)S(1)}, u32[]{:S(2)}, u32[]{:S(2)}) async-start(bf16[16,16,512]{2,1,0:T(8,128)(2,1)} %bitcast.4), calls=%async_computation.1 | async-start | bytes 524288 | tf_op jit(solution)/shard_map/all_to_all | solution.py:375
  28.6 3.3 %process_own.1 = (bf16[512,2048]{1,0:T(8,128)(2,1)S(1)}, bf16[512,512]{1,0:T(8,128)(2,1)S(1)}, f32[256,512]{1,0:T(8,128)S(1)}) custom-call(bf16[256,512]{1,0:T(8,128)(2,1)S(1)} %get-tuple-element.22.mid, f32[4,2048]{1,0:T(4,128)} %feats_any.3, s32[1,2048]{1,0:T(1,128)} %bitcast.8, f32[4,512]{1,0:T(4,128)} %feat_any.3, bf16[512,512]{1,0:T(8,128)(2,1)} %recv_any.3, ...), custom_call_target="tpu_custom_call" | custom-call | tf_op jit(solution)/shard_map/process_own/pallas_call | solution.py:287
  31.9 0.0 copy-start
  31.9 0.8 %copy-done = f32[256,512]{1,0:T(8,128)} copy-done((f32[256,512]{1,0:T(8,128)}, f32[256,512]{1,0:T(8,128)S(1)}, u32[]{:S(2)}) %copy-start) | copy-done | bytes 524312
  32.7 5.3 %all-to-all-done.1 = bf16[16,16,512]{2,1,0:T(8,128)(2,1)S(1)} async-done(((bf16[16,16,512]{2,1,0:T(8,128)(2,1)}), bf16[16,16,512]{2,1,0:T(8,128)(2,1)S(1)}, u32[]{:S(2)}, u32[]{:S(2)}) %all-to-all-start.1) | async-done | bytes 262176 | tf_op jit(solution)/shard_map/all_to_all | solution.py:375
  37.9 5.0 %process_rest.1 = bf16[256,512]{1,0:T(8,128)(2,1)} custom-call(bf16[256,512]{1,0:T(8,128)(2,1)S(1)} %get-tuple-element.22.mid, bf16[512,2048]{1,0:T(8,128)(2,1)S(1)} %get-tuple-element.23.pre, bf16[256,512]{1,0:T(8,128)(2,1)S(1)} %bitcast.7, bf16[512,512]{1,0:T(8,128)(2,1)S(1)} %get-tuple-element.25.w_out, s32[1]{0:T(128)S(6)} %copy.25.count_any, ...), custom_call_target="tpu_custom_call" | custom-call | tf_op jit(solution)/shard_map/process_rest/pallas_call | solution.py:287
Async XLA Ops:
  1.3 10.6 %collective-permute-start = (bf16[256,512]{1,0:T(8,128)(2,1)S(1)}, bf16[256,512]{1,0:T(8,128)(2,1)S(1)}, u32[]{:S(2)}, u32[]{:S(2)}) collective-permute-start(bf16[256,512]{1,0:T(8,128)(2,1)S(1)} %get-tuple-element.16.pair), channel_id=1, source_target_pairs={{0,1},{1,0},{2,3},{3,2},{4,5},{5,4},{6,7},{7,6},{8,9},{9,8},{10,11... | collective-permute-start | bytes 786440 | tf_op jit(solution)/shard_map/ppermute | solution.py:343
  1.8 10.1 %collective-permute-start.1 = (bf16[256,512]{1,0:T(8,128)(2,1)S(1)}, bf16[256,512]{1,0:T(8,128)(2,1)S(1)}, u32[]{:S(2)}, u32[]{:S(2)}) collective-permute-start(bf16[256,512]{1,0:T(8,128)(2,1)S(1)} %get-tuple-element.17.other), channel_id=1, source_target_pairs={{1,2},{2,1},{3,4},{4,3},{5,6},{6,5},{7,8},{8,7},{9,10},{10,9},{11,... | collective-permute-start | bytes 786440 | tf_op jit(solution)/shard_map/ppermute | solution.py:344
  2.5 17.7 %all-to-all-start = ((s32[16,1,16]{2,1,0:T(1,128)}), s32[16,1,16]{2,1,0:T(1,128)S(1)}, u32[]{:S(2)}, u32[]{:S(2)}) async-start(s32[16,1,16]{2,1,0:T(1,128)} %bitcast.13), calls=%async_computation | async-start | bytes 16384 | tf_op jit(solution)/shard_map/all_to_all | solution.py:324
  21.2 16.8 %all-to-all-start.1 = ((bf16[16,16,512]{2,1,0:T(8,128)(2,1)}), bf16[16,16,512]{2,1,0:T(8,128)(2,1)S(1)}, u32[]{:S(2)}, u32[]{:S(2)}) async-start(bf16[16,16,512]{2,1,0:T(8,128)(2,1)} %bitcast.4), calls=%async_computation.1 | async-start | bytes 524288 | tf_op jit(solution)/shard_map/all_to_all | solution.py:375
  31.9 0.8 %copy-start = (f32[256,512]{1,0:T(8,128)}, f32[256,512]{1,0:T(8,128)S(1)}, u32[]{:S(2)}) copy-start(f32[256,512]{1,0:T(8,128)S(1)} %get-tuple-element.26.first_any) | copy-start | bytes 1572868

commit v4 on v3

--- a/solution.py
+++ b/solution.py
@@ -218,13 +218,14 @@
 
 
 def process_own(
-    mid, feats_any, receiver_any, feat_any, recv_any, in_any, out_any, pre, w_out, first_any,
-    feats, receiver, w_feat, w_recv, w_in, first, recv_table, fa, wa, sems, out_sems,
+    mid, feats_any, sender_any, receiver_any, feat_any, recv_any, in_any, out_any,
+    pre, sender, receiver, w_out, first_any,
+    feats, w_feat, w_recv, w_in, first, recv_table, fa, wa, sems, out_sems,
 ):
     ready = fetch(
         (
             (feats_any, feats), (feat_any, w_feat), (recv_any, w_recv), (receiver_any, receiver),
-            (in_any.at[: w_in.shape[0], :], w_in), (out_any, w_out),
+            (in_any.at[: w_in.shape[0], :], w_in), (out_any, w_out), (sender_any, sender),
         ),
         sems,
     )
@@ -241,23 +242,21 @@
     ready(4)
     first[...] = mul(mid[...], w_in[...])
     fetch(((first, first_any),), out_sems)(0)
-    ready(5)
+    ready(5, 6)
 
 
 def process_rest(
-    mid, pre, listed, w_out, count_any, sender_any, receiver_any, first_any, in_any, node_any,
+    mid, pre, sender, receiver, listed, w_out, count_any, first_any, in_any, node_any,
     result_any,
-    count, sender, receiver, first, w_in, w_node, result, sems, out_sems,
+    count, first, w_in, w_node, result, sems, out_sems,
 ):
     ready = fetch(
         (
-            (sender_any, sender), (receiver_any, receiver), (count_any, count),
-            (first_any, first), (in_any.at[w_in.shape[0] :, :], w_in), (node_any, w_node),
+            (count_any, count), (first_any, first), (in_any.at[w_in.shape[0] :, :], w_in), (node_any, w_node),
         ),
         sems,
     )
     table = listed[...].T
-    ready(0, 1, 2)
 
     def to_of(i):
         return places(mid.shape[0], receiver[:, pl.ds(i * BLOCK, BLOCK)])
@@ -266,8 +265,9 @@
         span = pl.ds(i * BLOCK, BLOCK)
         return pre[:, span] + mul(table, places(table.shape[1], sender[:, span]))
 
+    ready(0)
     summed = summed_messages(sender.shape[1], pre_of, to_of, w_out, count[0])
-    ready(3, 4, 5)
+    ready(1, 2, 3)
     result[...] = nodes_of(mid[...], first[...], summed, w_in[...], w_node)
     fetch(((result, result_any),), out_sems)(0)
 
@@ -375,32 +375,34 @@
     listed = lax.all_to_all(
         outgoing.reshape(blocks, per, width), "tile", split_axis=0, concat_axis=0, tiled=True
     ).reshape(blocks * per, width)
-    pre, w_out, first = call(
+    pre, near_sender, near_receiver, w_out, first = call(
         process_own,
         "process_own",
         [mid],
-        [mesh_feats, mesh_receiver, w_proc_feat, w_proc_recv, w_proc_node_in, w_proc_out],
-        [shape(width, slots), square],
+        [
+            mesh_feats, mesh_sender, mesh_receiver, w_proc_feat, w_proc_recv, w_proc_node_in,
+            w_proc_out,
+        ],
+        [shape(width, slots), edge_index, edge_index, square],
         [shape(nodes, width, dtype=F32)],
         [
-            edge_feats, edge_index, feat_weight, square, square,
-            shape(nodes, width, dtype=F32), shape(width, nodes),
+            edge_feats, feat_weight, square, square, shape(nodes, width, dtype=F32),
+            shape(width, nodes),
         ]
         + stacked,
-        (6, 1),
+        (7, 1),
     )
     (result,) = call(
         process_rest,
         "process_rest",
-        [mid, pre, listed, w_out],
-        [mesh_count, mesh_sender, mesh_receiver, first, w_proc_node_in, w_proc_node_out],
+        [mid, pre, near_sender, near_receiver, listed, w_out],
+        [mesh_count, first, w_proc_node_in, w_proc_node_out],
         [],
         [node_rows],
         [
-            one, edge_index, edge_index, shape(nodes, width, dtype=F32), square, square,
-            node_rows,
+            one, shape(nodes, width, dtype=F32), square, square, node_rows,
         ],
-        (6, 1),
+        (4, 1),
     )
     return result
 

time: 43.6 us -> 43.3 us (level)
  no operation moved by 1% of the time
where the time goes in v4:
time: 43.3 us; the launch traced here: 43 us
  Pallas kernels  18.6 us (43%)
  starting transfers between devices  16.7 us (39%)
  waiting for transfers between devices  5.27 us (12%)
  between operations  1.54 us (4%)
  local copies, waits for them, and re-layouts  0.79 us (2%)
    pallas_call x5, Pallas kernels, call(): pl.pallas_call(kernel, out_shape=near_outs + far_outs, in_specs=[V] * len...  18.6 us
    all_to_all x1, starting transfers between devices, body(): lax.all_to_all(need_rows.reshape(blocks, 1, per), 'tile', split_axis=0, c...  8.8 us
    all_to_all x1, starting transfers between devices, body(): lax.all_to_all(outgoing.reshape(blocks, per, width), 'tile', split_axis=0...  6.74 us
    all_to_all x1, waiting for transfers between devices, body(): lax.all_to_all(outgoing.reshape(blocks, per, width), 'tile', split_axis=0...  5.26 us
  transfers between devices with their start and end apart: 4, of which 1 were waited for; matrix products, arithmetic and copies ran while one was open for 0% of the time, Pallas kernels for 27%

profile of v4, /device:TPU:0, one launch (start us, length us, event | category | flops | bytes accessed | tf_op | source)
XLA Modules:
  0.0 43.0 jit_solution(14272156964907682847)
XLA Ops:
  0.0 1.3 %band_ends.1 = (bf16[256,512]{1,0:T(8,128)(2,1)S(1)}, bf16[256,512]{1,0:T(8,128)(2,1)S(1)}, bf16[512,512]{1,0:T(8,128)(2,1)S(1)}, bf16[256,512]{1,0:T(8,128)(2,1...) custom-call(bf16[1024,512]{1,0:T(8,128)(2,1)} %grid_any.1, bf16[256,512]{1,0:T(8,128)(2,1)} %latent_any.1, ...), custom_call_target="tpu_custom_call" | custom-call | tf_op jit(solution)/shard_map/band_ends/pallas_call | solution.py:287
  1.3 0.5 %collective-permute-start = (bf16[256,512]{1,0:T(8,128)(2,1)S(1)}, bf16[256,512]{1,0:T(8,128)(2,1)S(1)}, u32[]{:S(2)}, u32[]{:S(2)}) collective-permute-start(bf16[256,512]{1,0:T(8,128)(2,1)S(1)} %get-tuple-element.18.pair), channel_id=1, source_target_pairs={{0,1},{1,0},{2,3},{3,2},{4,5},{5,4},{6,7},{7,6},{8,9},{9,8},{10,11... | collective-permute-start | bytes 786440 | tf_op jit(solution)/shard_map/ppermute | solution.py:343
  1.8 0.7 %collective-permute-start.1 = (bf16[256,512]{1,0:T(8,128)(2,1)S(1)}, bf16[256,512]{1,0:T(8,128)(2,1)S(1)}, u32[]{:S(2)}, u32[]{:S(2)}) collective-permute-start(bf16[256,512]{1,0:T(8,128)(2,1)S(1)} %get-tuple-element.19.other), channel_id=1, source_target_pairs={{1,2},{2,1},{3,4},{4,3},{5,6},{6,5},{7,8},{8,7},{9,10},{10,9},{11,... | collective-permute-start | bytes 786440 | tf_op jit(solution)/shard_map/ppermute | solution.py:344
  2.5 8.8 %all-to-all-start = ((s32[16,1,16]{2,1,0:T(1,128)}), s32[16,1,16]{2,1,0:T(1,128)S(1)}, u32[]{:S(2)}, u32[]{:S(2)}) async-start(s32[16,1,16]{2,1,0:T(1,128)} %bitcast.12), calls=%async_computation | async-start | bytes 16384 | tf_op jit(solution)/shard_map/all_to_all | solution.py:324
  12.0 0.0 collective-permute-done.from_pair
  12.0 0.0 collective-permute-done.1.from_other
  12.0 8.2 %encode.1 = (bf16[256,512]{1,0:T(8,128)(2,1)S(1)}, bf16[256,512]{1,0:T(8,128)(2,1)S(1)}) custom-call(bf16[256,512]{1,0:T(8,128)(2,1)S(1)} %collective-permute-done.from_pair, bf16[256,512]{1,0:T(8,128)(2,1)S(1)} %collective-permute-done.1.from_other, bf16[256,512]{1,0:T(8,128)(2,1)S(1)} %get-tuple-element.18.pair, ...), custom_call_target="tpu_custom_call" | custom-call | tf_op jit(solution)/shard_map/encode/pallas_call | solution.py:287
  20.2 0.0 all-to-all-done.asked
  20.2 1.0 %answer.1 = bf16[256,512]{1,0:T(8,128)(2,1)} custom-call(bf16[256,512]{1,0:T(8,128)(2,1)S(1)} %get-tuple-element.28.sent, s32[16,1,16]{2,1,0:T(1,128)S(1)} %all-to-all-done.asked), custom_call_target="tpu_custom_call" | custom-call | tf_op jit(solution)/shard_map/answer/pallas_call | solution.py:287
  21.2 6.7 %all-to-all-start.1 = ((bf16[16,16,512]{2,1,0:T(8,128)(2,1)}), bf16[16,16,512]{2,1,0:T(8,128)(2,1)S(1)}, u32[]{:S(2)}, u32[]{:S(2)}) async-start(bf16[16,16,512]{2,1,0:T(8,128)(2,1)} %bitcast.5), calls=%async_computation.1 | async-start | bytes 524288 | tf_op jit(solution)/shard_map/all_to_all | solution.py:375
  28.6 3.3 %process_own.1 = (bf16[512,2048]{1,0:T(8,128)(2,1)S(1)}, s32[1,2048]{1,0:T(1,128)S(1)}, s32[1,2048]{1,0:T(1,128)S(1)}, bf16[512,512]{1,0:T(8,128)(2,1)S(1)}, f32[256,512]{1,0:T(8,128)S(1)}) custom-call(bf16[256,512]{1,0:T(8,128)(2,1)S(1)} %get-tuple-element.24.mid, f32[4,2048]{1,0:T(4,128)} %feats_any.3, s32[1,2048]{1,0:T(1,128)} %bitcast.10, ...), custom_call_target="tpu_custom_call" | custom-call | tf_op jit(solution)/shard_map/process_own/pallas_call | solution.py:287
  31.9 0.0 copy-start
  31.9 0.8 %copy-done = f32[256,512]{1,0:T(8,128)} copy-done((f32[256,512]{1,0:T(8,128)}, f32[256,512]{1,0:T(8,128)S(1)}, u32[]{:S(2)}) %copy-start) | copy-done | bytes 524312
  32.7 5.3 %all-to-all-done.1 = bf16[16,16,512]{2,1,0:T(8,128)(2,1)S(1)} async-done(((bf16[16,16,512]{2,1,0:T(8,128)(2,1)}), bf16[16,16,512]{2,1,0:T(8,128)(2,1)S(1)}, u32[]{:S(2)}, u32[]{:S(2)}) %all-to-all-start.1) | async-done | bytes 262176 | tf_op jit(solution)/shard_map/all_to_all | solution.py:375
  37.9 4.8 %process_rest.1 = bf16[256,512]{1,0:T(8,128)(2,1)} custom-call(bf16[256,512]{1,0:T(8,128)(2,1)S(1)} %get-tuple-element.24.mid, bf16[512,2048]{1,0:T(8,128)(2,1)S(1)} %get-tuple-element.25.pre, s32[1,2048]{1,0:T(1,128)S(1)} %get-tuple-element.26.sender, s32[1,2048]{1,0:T(1,128)S(1)} %get-tuple-element.27.receiver, bf16[256,512]{1,0:T(8,128)(2,1)S(1)} %bitcast.7, ...), custom_call_target="tpu_custom_call" | custom-call | tf_op jit(solution)/shard_map/process_rest/pallas_call | solution.py:287
Async XLA Ops:
  1.3 10.6 %collective-permute-start = (bf16[256,512]{1,0:T(8,128)(2,1)S(1)}, bf16[256,512]{1,0:T(8,128)(2,1)S(1)}, u32[]{:S(2)}, u32[]{:S(2)}) collective-permute-start(bf16[256,512]{1,0:T(8,128)(2,1)S(1)} %get-tuple-element.18.pair), channel_id=1, source_target_pairs={{0,1},{1,0},{2,3},{3,2},{4,5},{5,4},{6,7},{7,6},{8,9},{9,8},{10,11... | collective-permute-start | bytes 786440 | tf_op jit(solution)/shard_map/ppermute | solution.py:343
  1.8 10.1 %collective-permute-start.1 = (bf16[256,512]{1,0:T(8,128)(2,1)S(1)}, bf16[256,512]{1,0:T(8,128)(2,1)S(1)}, u32[]{:S(2)}, u32[]{:S(2)}) collective-permute-start(bf16[256,512]{1,0:T(8,128)(2,1)S(1)} %get-tuple-element.19.other), channel_id=1, source_target_pairs={{1,2},{2,1},{3,4},{4,3},{5,6},{6,5},{7,8},{8,7},{9,10},{10,9},{11,... | collective-permute-start | bytes 786440 | tf_op jit(solution)/shard_map/ppermute | solution.py:344
  2.5 17.7 %all-to-all-start = ((s32[16,1,16]{2,1,0:T(1,128)}), s32[16,1,16]{2,1,0:T(1,128)S(1)}, u32[]{:S(2)}, u32[]{:S(2)}) async-start(s32[16,1,16]{2,1,0:T(1,128)} %bitcast.12), calls=%async_computation | async-start | bytes 16384 | tf_op jit(solution)/shard_map/all_to_all | solution.py:324
  21.2 16.8 %all-to-all-start.1 = ((bf16[16,16,512]{2,1,0:T(8,128)(2,1)}), bf16[16,16,512]{2,1,0:T(8,128)(2,1)S(1)}, u32[]{:S(2)}, u32[]{:S(2)}) async-start(bf16[16,16,512]{2,1,0:T(8,128)(2,1)} %bitcast.5), calls=%async_computation.1 | async-start | bytes 524288 | tf_op jit(solution)/shard_map/all_to_all | solution.py:375
  31.9 0.8 %copy-start = (f32[256,512]{1,0:T(8,128)}, f32[256,512]{1,0:T(8,128)S(1)}, u32[]{:S(2)}) copy-start(f32[256,512]{1,0:T(8,128)S(1)} %get-tuple-element.30.first_any) | copy-start | bytes 1572868

commit v5 on v4

--- a/solution.py
+++ b/solution.py
@@ -246,13 +246,13 @@
 
 
 def process_rest(
-    mid, pre, sender, receiver, listed, w_out, count_any, first_any, in_any, node_any,
+    count, mid, pre, sender, receiver, listed, w_out, first_any, in_any, node_any,
     result_any,
-    count, first, w_in, w_node, result, sems, out_sems,
+    first, w_in, w_node, result, sems, out_sems,
 ):
     ready = fetch(
         (
-            (count_any, count), (first_any, first), (in_any.at[w_in.shape[0] :, :], w_in), (node_any, w_node),
+            (first_any, first), (in_any.at[w_in.shape[0] :, :], w_in), (node_any, w_node),
         ),
         sems,
     )
@@ -265,9 +265,8 @@
         span = pl.ds(i * BLOCK, BLOCK)
         return pre[:, span] + mul(table, places(table.shape[1], sender[:, span]))
 
-    ready(0)
     summed = summed_messages(sender.shape[1], pre_of, to_of, w_out, count[0])
-    ready(1, 2, 3)
+    ready(0, 1, 2)
     result[...] = nodes_of(mid[...], first[...], summed, w_in[...], w_node)
     fetch(((result, result_any),), out_sems)(0)
 
@@ -283,11 +282,11 @@
     return jax.ShapeDtypeStruct(sizes, dtype)
 
 
-def call(kernel, name, near, far, near_outs, far_outs, scratch, copies):
+def call(kernel, name, near, far, near_outs, far_outs, scratch, copies, counts=()):
     return pl.pallas_call(
         kernel,
         out_shape=near_outs + far_outs,
-        in_specs=[V] * len(near) + [H] * len(far),
+        in_specs=[S] * len(counts) + [V] * len(near) + [H] * len(far),
         out_specs=[V] * len(near_outs) + [H] * len(far_outs),
         scratch_shapes=[
             (pltpu.SMEM if isinstance(s, Scalars) else pltpu.VMEM)(s.shape, s.dtype)
@@ -296,7 +295,7 @@
         + [pltpu.SemaphoreType.DMA((n,)) for n in copies],
         compiler_params=pltpu.CompilerParams(vmem_limit_bytes=48 * 2**20),
         name=name,
-    )(*near, *(x if x.size == 1 else pltpu.with_memory_space_constraint(x, pltpu.HBM) for x in far))
+    )(*counts, *near, *(x if x.size == 1 else pltpu.with_memory_space_constraint(x, pltpu.HBM) for x in far))
 
 
 def body(
@@ -396,13 +395,14 @@
         process_rest,
         "process_rest",
         [mid, pre, near_sender, near_receiver, listed, w_out],
-        [mesh_count, first, w_proc_node_in, w_proc_node_out],
+        [first, w_proc_node_in, w_proc_node_out],
         [],
         [node_rows],
         [
-            one, shape(nodes, width, dtype=F32), square, square, node_rows,
+            shape(nodes, width, dtype=F32), square, square, node_rows,
         ],
-        (4, 1),
+        (3, 1),
+        [mesh_count],
     )
     return result
 

time: 43.3 us -> 43.9 us (1.014)
  Pallas kernels: 18.6 us -> 19.2 us
    pallas_call x5, Pallas kernels: 18.6 us -> 19.2 us  [call(): pl.pallas_call(kernel, out_shape=near_outs + far_outs, in_specs=[S] * len...]
  transfers between devices with their start and end apart: 4 -> 4, of which waited for: 1 -> 1; matrix products, arithmetic and copies ran while one was open for 0% -> 0% of each run, Pallas kernels for 27% -> 26%
where the time goes in v5:
time: 43.9 us; the launch traced here: 43.5 us
  Pallas kernels  19.2 us (44%)
  starting transfers between devices  16.7 us (38%)
  waiting for transfers between devices  5.27 us (12%)
  between operations  1.54 us (4%)
  local copies, waits for them, and re-layouts  0.79 us (2%)
    pallas_call x5, Pallas kernels, call(): pl.pallas_call(kernel, out_shape=near_outs + far_outs, in_specs=[S] * len...  19.2 us
    all_to_all x1, starting transfers between devices, body(): lax.all_to_all(need_rows.reshape(blocks, 1, per), 'tile', split_axis=0, c...  8.8 us
    all_to_all x1, starting transfers between devices, body(): lax.all_to_all(outgoing.reshape(blocks, per, width), 'tile', split_axis=0...  6.74 us
    all_to_all x1, waiting for transfers between devices, body(): lax.all_to_all(outgoing.reshape(blocks, per, width), 'tile', split_axis=0...  5.26 us
  transfers between devices with their start and end apart: 4, of which 1 were waited for; matrix products, arithmetic and copies ran while one was open for 0% of the time, Pallas kernels for 26%

profile of v5, /device:TPU:0, one launch (start us, length us, event | category | flops | bytes accessed | tf_op | source)
XLA Modules:
  0.0 43.5 jit_solution(7053201020829432542)
XLA Ops:
  0.0 1.3 %band_ends.1 = (bf16[256,512]{1,0:T(8,128)(2,1)S(1)}, bf16[256,512]{1,0:T(8,128)(2,1)S(1)}, bf16[512,512]{1,0:T(8,128)(2,1)S(1)}, bf16[256,512]{1,0:T(8,128)(2,1...) custom-call(bf16[1024,512]{1,0:T(8,128)(2,1)} %grid_any.1, bf16[256,512]{1,0:T(8,128)(2,1)} %latent_any.1, ...), custom_call_target="tpu_custom_call" | custom-call | tf_op jit(solution)/shard_map/band_ends/pallas_call | solution.py:286
  1.3 0.5 %collective-permute-start = (bf16[256,512]{1,0:T(8,128)(2,1)S(1)}, bf16[256,512]{1,0:T(8,128)(2,1)S(1)}, u32[]{:S(2)}, u32[]{:S(2)}) collective-permute-start(bf16[256,512]{1,0:T(8,128)(2,1)S(1)} %get-tuple-element.18.pair), channel_id=1, source_target_pairs={{0,1},{1,0},{2,3},{3,2},{4,5},{5,4},{6,7},{7,6},{8,9},{9,8},{10,11... | collective-permute-start | bytes 786440 | tf_op jit(solution)/shard_map/ppermute | solution.py:342
  1.8 0.7 %collective-permute-start.1 = (bf16[256,512]{1,0:T(8,128)(2,1)S(1)}, bf16[256,512]{1,0:T(8,128)(2,1)S(1)}, u32[]{:S(2)}, u32[]{:S(2)}) collective-permute-start(bf16[256,512]{1,0:T(8,128)(2,1)S(1)} %get-tuple-element.19.other), channel_id=1, source_target_pairs={{1,2},{2,1},{3,4},{4,3},{5,6},{6,5},{7,8},{8,7},{9,10},{10,9},{11,... | collective-permute-start | bytes 786440 | tf_op jit(solution)/shard_map/ppermute | solution.py:343
  2.5 8.8 %all-to-all-start = ((s32[16,1,16]{2,1,0:T(1,128)}), s32[16,1,16]{2,1,0:T(1,128)S(1)}, u32[]{:S(2)}, u32[]{:S(2)}) async-start(s32[16,1,16]{2,1,0:T(1,128)} %bitcast.12), calls=%async_computation | async-start | bytes 16384 | tf_op jit(solution)/shard_map/all_to_all | solution.py:323
  12.0 0.0 collective-permute-done.from_pair
  12.0 0.0 collective-permute-done.1.from_other
  12.0 8.2 %encode.1 = (bf16[256,512]{1,0:T(8,128)(2,1)S(1)}, bf16[256,512]{1,0:T(8,128)(2,1)S(1)}) custom-call(bf16[256,512]{1,0:T(8,128)(2,1)S(1)} %collective-permute-done.from_pair, bf16[256,512]{1,0:T(8,128)(2,1)S(1)} %collective-permute-done.1.from_other, bf16[256,512]{1,0:T(8,128)(2,1)S(1)} %get-tuple-element.18.pair, ...), custom_call_target="tpu_custom_call" | custom-call | tf_op jit(solution)/shard_map/encode/pallas_call | solution.py:286
  20.2 0.0 all-to-all-done.asked
  20.2 1.0 %answer.1 = bf16[256,512]{1,0:T(8,128)(2,1)} custom-call(bf16[256,512]{1,0:T(8,128)(2,1)S(1)} %get-tuple-element.28.sent, s32[16,1,16]{2,1,0:T(1,128)S(1)} %all-to-all-done.asked), custom_call_target="tpu_custom_call" | custom-call | tf_op jit(solution)/shard_map/answer/pallas_call | solution.py:286
  21.2 6.7 %all-to-all-start.1 = ((bf16[16,16,512]{2,1,0:T(8,128)(2,1)}), bf16[16,16,512]{2,1,0:T(8,128)(2,1)S(1)}, u32[]{:S(2)}, u32[]{:S(2)}) async-start(bf16[16,16,512]{2,1,0:T(8,128)(2,1)} %bitcast.5), calls=%async_computation.1 | async-start | bytes 524288 | tf_op jit(solution)/shard_map/all_to_all | solution.py:374
  28.6 3.3 %process_own.1 = (bf16[512,2048]{1,0:T(8,128)(2,1)S(1)}, s32[1,2048]{1,0:T(1,128)S(1)}, s32[1,2048]{1,0:T(1,128)S(1)}, bf16[512,512]{1,0:T(8,128)(2,1)S(1)}, f32[256,512]{1,0:T(8,128)S(1)}) custom-call(bf16[256,512]{1,0:T(8,128)(2,1)S(1)} %get-tuple-element.24.mid, f32[4,2048]{1,0:T(4,128)} %feats_any.3, s32[1,2048]{1,0:T(1,128)} %bitcast.10, ...), custom_call_target="tpu_custom_call" | custom-call | tf_op jit(solution)/shard_map/process_own/pallas_call | solution.py:286
  31.9 0.0 copy-start
  31.9 0.8 %copy-done = f32[256,512]{1,0:T(8,128)} copy-done((f32[256,512]{1,0:T(8,128)}, f32[256,512]{1,0:T(8,128)S(1)}, u32[]{:S(2)}) %copy-start) | copy-done | bytes 524312
  32.7 5.3 %all-to-all-done.1 = bf16[16,16,512]{2,1,0:T(8,128)(2,1)S(1)} async-done(((bf16[16,16,512]{2,1,0:T(8,128)(2,1)}), bf16[16,16,512]{2,1,0:T(8,128)(2,1)S(1)}, u32[]{:S(2)}, u32[]{:S(2)}) %all-to-all-start.1) | async-done | bytes 262176 | tf_op jit(solution)/shard_map/all_to_all | solution.py:374
  37.9 5.4 %process_rest.1 = bf16[256,512]{1,0:T(8,128)(2,1)} custom-call(s32[1]{0:T(128)S(6)} %copy.25.count, bf16[256,512]{1,0:T(8,128)(2,1)S(1)} %get-tuple-element.24.mid, bf16[512,2048]{1,0:T(8,128)(2,1)S(1)} %get-tuple-element.25.pre, s32[1,2048]{1,0:T(1,128)S(1)} %get-tuple-element.26.sender, s32[1,2048]{1,0:T(1,128)S(1)} %get-tuple-element.27.receiver, ...), custom_call_target="tpu_custom_call" | custom-call | tf_op jit(solution)/shard_map/process_rest/pallas_call | solution.py:286
Async XLA Ops:
  1.3 10.6 %collective-permute-start = (bf16[256,512]{1,0:T(8,128)(2,1)S(1)}, bf16[256,512]{1,0:T(8,128)(2,1)S(1)}, u32[]{:S(2)}, u32[]{:S(2)}) collective-permute-start(bf16[256,512]{1,0:T(8,128)(2,1)S(1)} %get-tuple-element.18.pair), channel_id=1, source_target_pairs={{0,1},{1,0},{2,3},{3,2},{4,5},{5,4},{6,7},{7,6},{8,9},{9,8},{10,11... | collective-permute-start | bytes 786440 | tf_op jit(solution)/shard_map/ppermute | solution.py:342
  1.8 10.1 %collective-permute-start.1 = (bf16[256,512]{1,0:T(8,128)(2,1)S(1)}, bf16[256,512]{1,0:T(8,128)(2,1)S(1)}, u32[]{:S(2)}, u32[]{:S(2)}) collective-permute-start(bf16[256,512]{1,0:T(8,128)(2,1)S(1)} %get-tuple-element.19.other), channel_id=1, source_target_pairs={{1,2},{2,1},{3,4},{4,3},{5,6},{6,5},{7,8},{8,7},{9,10},{10,9},{11,... | collective-permute-start | bytes 786440 | tf_op jit(solution)/shard_map/ppermute | solution.py:343
  2.5 17.7 %all-to-all-start = ((s32[16,1,16]{2,1,0:T(1,128)}), s32[16,1,16]{2,1,0:T(1,128)S(1)}, u32[]{:S(2)}, u32[]{:S(2)}) async-start(s32[16,1,16]{2,1,0:T(1,128)} %bitcast.12), calls=%async_computation | async-start | bytes 16384 | tf_op jit(solution)/shard_map/all_to_all | solution.py:323
  21.2 16.8 %all-to-all-start.1 = ((bf16[16,16,512]{2,1,0:T(8,128)(2,1)}), bf16[16,16,512]{2,1,0:T(8,128)(2,1)S(1)}, u32[]{:S(2)}, u32[]{:S(2)}) async-start(bf16[16,16,512]{2,1,0:T(8,128)(2,1)} %bitcast.5), calls=%async_computation.1 | async-start | bytes 524288 | tf_op jit(solution)/shard_map/all_to_all | solution.py:374
  31.9 0.8 %copy-start = (f32[256,512]{1,0:T(8,128)}, f32[256,512]{1,0:T(8,128)S(1)}, u32[]{:S(2)}) copy-start(f32[256,512]{1,0:T(8,128)S(1)} %get-tuple-element.30.first_any) | copy-start | bytes 1572868
